TPU v7x, 512 devices: a whole 4x8x8 slice. The times are simulated.
512 devices in a mesh: fsdp: 64 (over y, z), tp: 8 (over x, core).
Axes of the slice: x: 4, y: 8, z: 8, core: 2. Of those that a mesh axis runs over, the one named last changes fastest.
Arguments:
- gradient: bfloat16 [8192, 14336], P('fsdp', 'tp'), may hold values from -50 to 50
- momentum: float32 [8192, 14336], P('fsdp', 'tp'), may hold values from -5 to 5
- right_factor: bfloat16 [14336, 512], P(('tp', 'fsdp')), may hold values from -6 to 6
Outputs:
- update: bfloat16 [8192, 14336], P('fsdp', 'tp')
- momentum_new: float32 [8192, 14336], P('fsdp', 'tp')
- factor_new: bfloat16 [14336, 512], P(('tp', 'fsdp'))
All inputs are finite; a program needn't handle non-finite values.
Results may differ from a plain program's by a relative error of at most 0.015.
Values may be sent and summed in bfloat16 or wider, within the bound.
A program may use at most 64 MiB of HBM per device.

v0:
```python
import math

import jax
import jax.numpy as jnp
from jax import lax
from jax.sharding import PartitionSpec as P

D = 8192
FFW = 14336
RANK = 512


def body(gradient, momentum, right_factor):
    whole = momentum + gradient.astype(jnp.float32)
    wide = whole.astype(jnp.bfloat16)
    row_count = wide.shape[0]
    columns = wide
    partial_value = jnp.dot(
        columns,
        lax.all_gather(right_factor, "fsdp", axis=0, tiled=True),
        preferred_element_type=jnp.float32,
    )
    left = lax.psum(partial_value, "tp")
    gram = lax.psum(jnp.dot(left.T, left, precision=lax.Precision.HIGHEST), "fsdp")
    lower = jnp.linalg.cholesky(gram)
    ortho = jax.scipy.linalg.solve_triangular(lower, left.T, lower=True).T.astype(jnp.bfloat16)
    columns = wide
    right = lax.psum_scatter(
        lax.dot_general(
            columns, ortho, (((0,), (0,)), ((), ())), preferred_element_type=jnp.float32
        ),
        "fsdp",
        scatter_dimension=0,
        tiled=True,
    )
    right_b = right.astype(jnp.bfloat16)
    dims = (((1,), (1,)), ((), ()))
    right_f = right_b.astype(jnp.float32)
    squares = jnp.sum(right_f * right_f, axis=0)
    norms = jnp.sqrt(lax.psum(squares, ("fsdp", "tp")) + 1e-06)
    factor_new = (math.sqrt(FFW) * right_f / norms).astype(jnp.bfloat16)
    scaled = (ortho.astype(jnp.float32) * (norms / math.sqrt(FFW))).astype(jnp.bfloat16)
    stacked = jnp.concatenate([ortho, scaled], axis=0)
    combined = lax.dot_general(
        stacked,
        lax.all_gather(factor_new, "fsdp", axis=0, tiled=True),
        dims,
        preferred_element_type=jnp.float32,
    )
    update = (math.sqrt(D / RANK) * combined[:row_count]).astype(jnp.bfloat16)
    momentum_new = whole - 0.05 * combined[row_count:]
    return (update, momentum_new, factor_new)


def solution(mesh):
    return jax.shard_map(
        body,
        mesh=mesh,
        in_specs=(P("fsdp", "tp"), P("fsdp", "tp"), P(("tp", "fsdp"), None)),
        out_specs=(P("fsdp", "tp"), P("fsdp", "tp"), P(("tp", "fsdp"), None)),
        check_vma=False,
    )
```

profile of v0, /device:TPU:6, one launch (start us, length us, event | category | flops | bytes accessed | tf_op | source)
XLA Modules:
  0.0 781.1 jit_solution(10168177194077443276)
XLA Ops:
  8.0 91.4 %all-gather.5.cloned.1.call-done = bf16[64,28,512]{2,1,0:T(8,128)(2,1)} async-done(((bf16[1,28,512]{2,1,0:T(8,128)(2,1)}), bf16[64,28,512]{2,1,0:T(8,128)(2,1)}) %all-gather.5.cloned.1.call-update) | async-done | bytes 1835024 | tf_op jit(solution)/shard_map/all_gather | solution.py:20
  103.1 65.1 %all-reduce.6.cloned.1.call-done = f32[128,512]{1,0:T(8,128)} async-done(((f32[128,512]{1,0:T(8,128)}), f32[128,512]{1,0:T(8,128)}) %all-reduce.6.cloned.1.call-update) | async-done | bytes 262160 | tf_op jit(solution)/shard_map/psum | solution.py:23
  168.2 3.1 fusion.52
  171.4 161.8 %all-reduce.8.cloned.1.call-done = f32[512,512]{0,1:T(8,128)} async-done(((f32[512,512]{0,1:T(8,128)}), f32[512,512]{0,1:T(8,128)}) %all-reduce.8.cloned.1.call-update) | async-done | bytes 1048592 | tf_op jit(solution)/shard_map/psum | solution.py:24
  336.1 11.7 %cholesky.104 = f32[128,128]{1,0:T(8,128)S(1)} custom-call(f32[128,128]{1,0:T(8,128)S(1)} %cholesky.266), custom_call_target="Cholesky" | custom-call | tf_op jit(solution)/shard_map/jit(cholesky)/cholesky | solution.py:25
  347.8 9.8 %custom-call.31 = f32[1,128,128]{1,2,0:T(8,128)S(1)} custom-call(f32[1,128,128]{2,1,0:T(8,128)S(1)} %get-tuple-element.39), custom_call_target="InvertDiagBlocksLowerTriangular" | custom-call | tf_op jit(solution)/shard_map/jit(cholesky)/cholesky | solution.py:25
  360.3 11.7 %cholesky.217 = f32[128,128]{1,0:T(8,128)S(1)} custom-call(f32[128,128]{1,0:T(8,128)S(1)} %cholesky.270), custom_call_target="Cholesky" | custom-call | tf_op jit(solution)/shard_map/jit(cholesky)/cholesky | solution.py:25
  372.1 10.0 %custom-call.32 = f32[1,128,128]{1,2,0:T(8,128)S(1)} custom-call(f32[1,128,128]{2,1,0:T(8,128)S(1)} %get-tuple-element.36), custom_call_target="InvertDiagBlocksLowerTriangular" | custom-call | tf_op jit(solution)/shard_map/jit(cholesky)/cholesky | solution.py:25
  383.6 11.7 %cholesky.238 = f32[128,128]{1,0:T(8,128)S(1)} custom-call(f32[128,128]{1,0:T(8,128)S(1)} %cholesky.275), custom_call_target="Cholesky" | custom-call | tf_op jit(solution)/shard_map/jit(cholesky)/cholesky | solution.py:25
  396.1 9.8 %custom-call.33 = f32[1,128,128]{1,2,0:T(8,128)S(1)} custom-call(f32[1,128,128]{2,1,0:T(8,128)S(1)} %get-tuple-element.33), custom_call_target="InvertDiagBlocksLowerTriangular" | custom-call | tf_op jit(solution)/shard_map/jit(cholesky)/cholesky | solution.py:25
  407.3 11.7 %cholesky.255 = f32[128,128]{1,0:T(8,128)S(1)} custom-call(f32[128,128]{1,0:T(8,128)S(1)} %convolution_subtract_fusion.5), custom_call_target="Cholesky" | custom-call | tf_op jit(solution)/shard_map/jit(cholesky)/cholesky | solution.py:25
  423.2 10.9 %while.1 = (s32[]{:T(128)}, f32[512,512]{1,0:T(8,128)S(1)}, s32[4,2]{0,1:T(2,128)S(1)}, f32[4,128,128]{2,1,0:T(8,128)}, s32[]{:T(128)}) while((s32[]{:T(128)}, f32[512,512]{1,0:T(8,128)S(1)}, s32[4,2]{0,1:T(2,128)S(1)}, f32[4,128,128]{2,1,0:T(8,128)}, s32[]{:T(128)}) %tuple.42), condition=%wide.while_cond, body=%wide.while_body.sunk | while | flops 2 | bytes 132205 | solution.py:26
  434.2 40.1 %custom-call.34 = f32[4,128,128]{1,2,0:T(8,128)S(1)} custom-call(f32[4,128,128]{2,1,0:T(8,128)} %get-tuple-element.10), custom_call_target="InvertDiagBlocksLowerTriangular" | custom-call | tf_op jit(solution)/shard_map/jit(_solve_triangular)/triangular_solve | solution.py:26
  482.5 76.8 %fusion = f32[32,512]{1,0:T(8,128)S(1)} fusion(f32[1792,512]{1,0:T(8,128)} %fusion.38), kind=kCustom, calls=%all-reduce-scatter | all-reduce-scatter fusion | flops 1048577 | bytes 3737600
  559.4 3.0 collective-permute-start.1
  562.4 4.4 collective-permute-start.2
  566.8 2.8 collective-permute-start.7
  569.6 5.8 collective-permute-start.3
  575.4 4.7 collective-permute-start.4
  580.1 6.0 collective-permute-start.5
  586.1 3.4 collective-permute-start.6
  589.5 3.2 collective-permute-start
  595.9 94.9 %psum.23 = f32[512]{0:T(512)S(1)} all-reduce(f32[512]{0:T(512)S(1)} %fusion.25), channel_id=1, replica_groups=mesh['fsdp'=64,'tp'=8] {'fsdp','tp'}, use_global_device_ids=true, to_apply=%region_12.13 | all-reduce | flops 512 | bytes 4096 | tf_op jit(solution)/shard_map/psum | solution.py:40
  692.3 77.8 %all-gather.7.cloned.1.call-done = bf16[64,28,512]{2,1,0:T(8,128)(2,1)} async-done(((bf16[1,28,512]{2,1,0:T(8,128)(2,1)}), bf16[64,28,512]{2,1,0:T(8,128)(2,1)}) %all-gather.7.cloned.1.call-update) | async-done | bytes 1835024 | tf_op jit(solution)/shard_map/all_gather | solution.py:46
  (82 shorter events, 42.9 us)
Async XLA Ops:
  7.2 92.2 %all-gather.5.cloned.1.call-start = ((), (), s32[]{:S(2)}) async-start(), calls=%async_computation.2 | async-start | bytes 2129920 | tf_op jit(solution)/shard_map/all_gather | solution.py:20
  7.9 94.0 %copy-start = (f32[128,1792]{1,0:T(8,128)S(1)}, f32[128,1792]{1,0:T(8,128)}, u32[]{:S(2)}) copy-start(f32[128,1792]{1,0:T(8,128)} %param.4) | copy-start | bytes 2752516
  7.9 94.0 %copy-start.2 = (bf16[128,1792]{1,0:T(8,128)(2,1)S(1)}, bf16[128,1792]{1,0:T(8,128)(2,1)}, u32[]{:S(2)}) copy-start(bf16[128,1792]{1,0:T(8,128)(2,1)} %param.3) | copy-start | bytes 1376260
  7.9 160.3 %all-reduce.6.cloned.1.call-start = ((), (), s32[]{:S(2)}) async-start(), calls=%async_computation | async-start | bytes 524288 | tf_op jit(solution)/shard_map/psum | solution.py:23
  103.0 230.2 %all-reduce.8.cloned.1.call-start = ((), (), s32[]{:S(2)}) async-start(), calls=%async_computation.1 | async-start | bytes 2097152 | tf_op jit(solution)/shard_map/psum | solution.py:24
  171.3 598.8 %all-gather.7.cloned.1.call-start = ((), (), s32[]{:S(2)}) async-start(), calls=%async_computation.3 | async-start | bytes 2129920 | tf_op jit(solution)/shard_map/all_gather | solution.py:46
  333.2 1.7 copy-start.1
  335.1 1.0 copy-start.3
  559.4 26.7 %collective-permute-start.1 = (bf16[32,512]{1,0:T(8,128)(2,1)S(1)}, bf16[32,512]{1,0:T(8,128)(2,1)S(1)}, u32[]{:S(2)}, u32[]{:S(2)}) collective-permute-start(bf16[32,512]{1,0:T(8,128)(2,1)S(1)} %convert.40), channel_id=1, source_target_pairs={{0,16},{8,24},{16,32},{24,40},{32,48},{40,56},{48,64},{56,72},{64,... | collective-permute-start | bytes 98312
  562.4 27.1 %collective-permute-start.2 = (bf16[32,512]{1,0:T(8,128)(2,1)S(1)}, bf16[32,512]{1,0:T(8,128)(2,1)S(1)}, u32[]{:S(2)}, u32[]{:S(2)}) collective-permute-start(bf16[32,512]{1,0:T(8,128)(2,1)S(1)} %convert.40), channel_id=1, source_target_pairs={{0,24},{8,32},{16,40},{24,48},{32,56},{40,64},{48,72},{56,80},{64,... | collective-permute-start | bytes 98312
  566.8 13.3 %collective-permute-start.7 = (bf16[28,512]{1,0:T(8,128)(2,1)S(1)}, bf16[28,512]{1,0:T(8,128)(2,1)S(1)}, u32[]{:S(2)}, u32[]{:S(2)}) collective-permute-start(bf16[28,512]{1,0:T(8,128)(2,1)S(1)} %slice.135), channel_id=1, source_target_pairs={{0,64},{8,72},{16,80},{24,88},{32,96},{40,104},{48,112},{56,120},{... | collective-permute-start | bytes 86024
  569.6 25.0 %collective-permute-start.3 = (bf16[32,512]{1,0:T(8,128)(2,1)S(1)}, bf16[32,512]{1,0:T(8,128)(2,1)S(1)}, u32[]{:S(2)}, u32[]{:S(2)}) collective-permute-start(bf16[32,512]{1,0:T(8,128)(2,1)S(1)} %convert.40), channel_id=1, source_target_pairs={{0,32},{8,40},{16,48},{24,56},{32,64},{40,72},{48,80},{56,88},{64,... | collective-permute-start | bytes 98312
  575.4 19.2 %collective-permute-start.4 = (bf16[32,512]{1,0:T(8,128)(2,1)S(1)}, bf16[32,512]{1,0:T(8,128)(2,1)S(1)}, u32[]{:S(2)}, u32[]{:S(2)}) collective-permute-start(bf16[32,512]{1,0:T(8,128)(2,1)S(1)} %convert.40), channel_id=1, source_target_pairs={{0,40},{8,48},{16,56},{24,64},{32,72},{40,80},{48,88},{56,96},{64,... | collective-permute-start | bytes 98312
  580.1 14.5 %collective-permute-start.5 = (bf16[32,512]{1,0:T(8,128)(2,1)S(1)}, bf16[32,512]{1,0:T(8,128)(2,1)S(1)}, u32[]{:S(2)}, u32[]{:S(2)}) collective-permute-start(bf16[32,512]{1,0:T(8,128)(2,1)S(1)} %convert.40), channel_id=1, source_target_pairs={{0,48},{8,56},{16,64},{24,72},{32,80},{40,88},{48,96},{56,104},{64... | collective-permute-start | bytes 98312
  586.1 8.5 %collective-permute-start.6 = (bf16[32,512]{1,0:T(8,128)(2,1)S(1)}, bf16[32,512]{1,0:T(8,128)(2,1)S(1)}, u32[]{:S(2)}, u32[]{:S(2)}) collective-permute-start(bf16[32,512]{1,0:T(8,128)(2,1)S(1)} %convert.40), channel_id=1, source_target_pairs={{0,56},{8,64},{16,72},{24,80},{32,88},{40,96},{48,104},{56,112},{6... | collective-permute-start | bytes 98312
  589.5 5.2 collective-permute-start
Sparse Core Ops, SparseCore 0:
  11.0 88.3 all-gather.4
  103.1 65.0 all-reduce.5
  171.7 161.4 all-reduce.7
  691.6 78.4 all-gather.6
where the time goes:
time: 782 us; the launch traced here: 781 us
  waiting for transfers between devices  397 us (51%)
  blocking collectives  172 us (22%)
  other arithmetic  122 us (16%)
  starting transfers between devices  33.4 us (4%)
  local copies, waits for them, and re-layouts  21.1 us (3%)
  matrix products  18.5 us (2%)
  between operations  17.4 us (2%)
    psum x1, waiting for transfers between devices, body(): lax.psum(jnp.dot(left.T, left, precision=lax.Precision.HIGHEST), 'fsdp')  162 us
    psum x1, blocking collectives, body(): norms = jnp.sqrt(lax.psum(squares, ('fsdp', 'tp')) + 1e-06)  94.9 us
    all_gather x1, waiting for transfers between devices, body(): lax.all_gather(right_factor, 'fsdp', axis=0, tiled=True)  91.4 us
    another operation x14, other arithmetic, body(): lower = jnp.linalg.cholesky(gram)  78.6 us
    all_gather x1, waiting for transfers between devices, body(): lax.all_gather(factor_new, 'fsdp', axis=0, tiled=True)  77.8 us
    unnamed x1, blocking collectives  76.8 us
    psum x1, waiting for transfers between devices, body(): left = lax.psum(partial_value, 'tp')  65.1 us
    another operation x3, other arithmetic, body(): jax.scipy.linalg.solve_triangular(lower, left.T, lower=True)  40.5 us
  transfers between devices with their start and end apart: 12, of which 4 were waited for; matrix products, arithmetic and copies ran while one was open for 0% of the time, Pallas kernels for 0%

commit v1 on v0

v1 whole, which is shorter than its diff:
```python
import functools
import math

import jax
import jax.numpy as jnp
from jax import lax
from jax.experimental import pallas as pl
from jax.experimental.pallas import tpu as pltpu
from jax.sharding import PartitionSpec as P

D = 8192
FFW = 14336
RANK = 512
N = 8
ROWS = 28
PAD = 32
HALF = 16
PARTS = 2
WIDTH = N // PARTS
MESH = pl.DeviceIdType.MESH
HIGHEST = lax.Precision.HIGHEST
VMEM = pl.BlockSpec(memory_space=pltpu.VMEM)


def params(collective_id):
    return pltpu.CompilerParams(
        collective_id=collective_id, has_side_effects=True, vmem_limit_bytes=48 * 2**20
    )


def wrap(index):
    return lax.rem(index + 2 * N, N)


def greet(peers):
    barrier = pltpu.get_barrier_semaphore()
    for peer in peers:
        pl.semaphore_signal(barrier, inc=1, device_id=peer, device_id_type=MESH)
    pl.semaphore_wait(barrier, len(peers))


def remote(src, dst, send_sem, recv_sem, device):
    return pltpu.make_async_remote_copy(
        src_ref=src, dst_ref=dst, send_sem=send_sem, recv_sem=recv_sem,
        device_id=device, device_id_type=MESH,
    )


def place():
    fsdp = lax.axis_index("fsdp")
    return fsdp // N, lax.rem(fsdp, N), lax.axis_index("tp")


def line_device(axis, offset):
    y, z, tp = place()
    if axis == 0:
        return (wrap(y + offset) * N + z, tp)
    return (y * N + wrap(z + offset), tp)


def plane_peers():
    return [line_device(axis, k) for axis in range(2) for k in range(1, N)]


def chain_length(direction, part):
    return N // 2 if direction == part else N // 2 - 1


CHAINS = [(h, d, p) for h in range(2) for d in range(2) for p in range(PARTS)]


def gather_plane(x_ref, out_ref, sems):
    send1, recv1, send2, recv2 = sems
    y, z, _ = place()
    ring = (y, z)
    sends = []
    for k in range(1, N):
        for h in range(2):
            rows = pl.ds(h * HALF, HALF)
            copy = remote(
                x_ref.at[rows], out_ref.at[y, z, rows],
                send1.at[h, k], recv1.at[h, k], line_device(1 - h, k),
            )
            copy.start()
            sends.append(copy)
    out_ref[y, z] = x_ref[...]
    for copy in sends:
        copy.wait_recv()

    def slot(h, index, part):
        part = pl.ds(part * WIDTH, WIDTH)
        rows = pl.ds(h * HALF, HALF)
        return out_ref.at[index, part, rows] if h == 0 else out_ref.at[part, index, rows]

    arriving = {}
    for step in range(1, N // 2 + 2):
        for h, d, p in CHAINS:
            sign = 1 - 2 * d
            if (h, d, p, step - 1) in arriving:
                arriving[h, d, p, step - 1].wait_recv()
            if step <= chain_length(d, p):
                ref = slot(h, wrap(ring[h] - sign * (step - 1)), p)
                copy = remote(
                    ref, ref, send2.at[h, d, step, p], recv2.at[h, d, step, p],
                    line_device(h, sign),
                )
                copy.start()
                sends.append(copy)
                arriving[h, d, p, step] = copy
    for copy in sends:
        copy.wait_send()


GATHER_SEMS = [
    pltpu.SemaphoreType.DMA((2, N)),
    pltpu.SemaphoreType.DMA((2, N)),
    pltpu.SemaphoreType.DMA((2, 2, N // 2 + 1, PARTS)),
    pltpu.SemaphoreType.DMA((2, 2, N // 2 + 1, PARTS)),
]


def gather_kernel(x_ref, out_ref, *sems):
    greet(plane_peers())
    gather_plane(x_ref, out_ref, sems)


def gather(x):
    return pl.pallas_call(
        gather_kernel,
        out_shape=jax.ShapeDtypeStruct((N, N, PAD, RANK), jnp.bfloat16),
        in_specs=[VMEM],
        out_specs=VMEM,
        scratch_shapes=list(GATHER_SEMS),
        compiler_params=params(0),
        name="gather_factor",
    )(x)


def tp_device(offset):
    return (lax.axis_index("fsdp"), wrap(lax.axis_index("tp") + offset))


def left_kernel(x_ref, out_ref, landed, send1, recv1, send2, recv2):
    tp = lax.axis_index("tp")
    greet([tp_device(k) for k in range(1, N)])

    def rows(index):
        return pl.ds(pl.multiple_of(index * HALF, HALF), HALF)

    copies = []
    for k in range(1, N):
        copy = remote(
            x_ref.at[rows(wrap(tp + k))], landed.at[k], send1.at[k], recv1.at[k], tp_device(k)
        )
        copy.start()
        copies.append(copy)
    total = x_ref[rows(tp), :]
    for k, copy in enumerate(copies):
        copy.wait_recv()
        total = total + landed[k + 1]
    out_ref[rows(tp), :] = total
    second = []
    for k in range(1, N):
        copy = remote(
            out_ref.at[rows(tp)], out_ref.at[rows(tp)], send2.at[k], recv2.at[k], tp_device(k)
        )
        copy.start()
        second.append(copy)
    for copy in second:
        copy.wait_recv()
    for copy in copies + second:
        copy.wait_send()


def sum_left(partial_value):
    return pl.pallas_call(
        left_kernel,
        out_shape=jax.ShapeDtypeStruct(partial_value.shape, jnp.float32),
        in_specs=[VMEM],
        out_specs=VMEM,
        scratch_shapes=[pltpu.VMEM((N, HALF, RANK), jnp.float32)]
        + [pltpu.SemaphoreType.DMA((N,)) for _ in range(4)],
        compiler_params=params(1),
        name="sum_left",
    )(partial_value)


def gram_kernel(gram_ref, out_ref, landed1, landed2, mine, send1, recv1, send2, recv2, send3, recv3):
    y, z, tp = place()
    greet(plane_peers())
    copies = []
    for k in range(1, N):
        row = pl.multiple_of(tp * (RANK // N) + wrap(z + k) * N, N)
        copy = remote(
            gram_ref.at[pl.ds(row, N)], landed1.at[k], send1.at[k], recv1.at[k], line_device(1, k)
        )
        copy.start()
        copies.append(copy)
    total = gram_ref[pl.ds(pl.multiple_of(tp * (RANK // N) + z * N, N), N), :]
    for k, copy in enumerate(copies):
        copy.wait_recv()
        total = total + landed1[k + 1]
    landed2[y] = total
    mine[...] = total
    second = []
    for k in range(1, N):
        copy = remote(mine, landed2.at[y], send2.at[k], recv2.at[k], line_device(0, k))
        copy.start()
        second.append(copy)
    for copy in second:
        copy.wait_recv()
    total = landed2[0]
    for k in range(1, N):
        total = total + landed2[k]
    rows = pl.ds(pl.multiple_of(z * N, N), N)
    out_ref[rows, :] = total
    third = []
    for k in range(1, N):
        copy = remote(out_ref.at[rows], out_ref.at[rows], send3.at[k], recv3.at[k], line_device(1, k))
        copy.start()
        third.append(copy)
    for copy in third:
        copy.wait_recv()
    for copy in copies + second + third:
        copy.wait_send()


def sum_gram(gram):
    return pl.pallas_call(
        gram_kernel,
        out_shape=jax.ShapeDtypeStruct((RANK // N, RANK), jnp.float32),
        in_specs=[VMEM],
        out_specs=VMEM,
        scratch_shapes=[
            pltpu.VMEM((N, N, RANK), jnp.float32),
            pltpu.VMEM((N, N, RANK), jnp.float32),
            pltpu.VMEM((N, RANK), jnp.float32),
        ]
        + [pltpu.SemaphoreType.DMA((N,)) for _ in range(6)],
        compiler_params=params(2),
        name="sum_gram",
    )(gram)


def spread_kernel(x_ref, out_ref, send1, recv1, send2, recv2):
    tp = lax.axis_index("tp")
    fsdp = lax.axis_index("fsdp")
    size = RANK // N
    sibling = (fsdp, tp + 1 - 2 * lax.rem(tp, 2))
    greet([tp_device(2), tp_device(4), tp_device(6), sibling])

    def rows(index):
        return pl.ds(pl.multiple_of(index * size, size), size)

    copies = []
    for k in range(1, N // 2):
        copy = remote(
            x_ref, out_ref.at[rows(tp)], send1.at[k], recv1.at[k], tp_device(2 * k)
        )
        copy.start()
        copies.append(copy)
    near = [remote(x_ref, out_ref.at[rows(tp)], send2.at[0], recv2.at[0], sibling)]
    near[0].start()
    out_ref[rows(tp), :] = x_ref[...]
    for k in (1, 3, 2):
        copies[k - 1].wait_recv()
        ref = out_ref.at[rows(wrap(tp - 2 * k))]
        copy = remote(ref, ref, send2.at[k], recv2.at[k], sibling)
        copy.start()
        near.append(copy)
    for copy in near:
        copy.wait_recv()
    for copy in copies + near:
        copy.wait_send()


def spread_gram(x):
    return pl.pallas_call(
        spread_kernel,
        out_shape=jax.ShapeDtypeStruct((RANK, RANK), jnp.float32),
        in_specs=[VMEM],
        out_specs=VMEM,
        scratch_shapes=[pltpu.SemaphoreType.DMA((N // 2,)) for _ in range(4)],
        compiler_params=params(3),
        name="spread_gram",
    )(x)


BLOCK = 128
BASE = 8


def small_inverse(panel, first):
    wide = (BASE, BLOCK)
    entry = {
        (i, j): jnp.broadcast_to(panel[i : i + 1, first + j : first + j + 1], wide)
        for i in range(BASE)
        for j in range(i + 1)
    }
    lower, inverse, scale = {}, {}, {}
    for j in range(BASE):
        pivot = entry[j, j]
        guess = lax.rsqrt(pivot)
        scale[j] = guess * (1.5 - 0.5 * ((pivot * guess) * guess))
        for i in range(j + 1, BASE):
            lower[i, j] = entry[i, j] * scale[j]
        for i in range(j + 1, BASE):
            for m in range(j + 1, i + 1):
                entry[i, m] = entry[i, m] - lower[i, j] * lower[m, j]
    for j in range(BASE):
        inverse[j, j] = scale[j]
        for i in range(j + 1, BASE):
            total = lower[i, j] * inverse[j, j]
            for m in range(j + 1, i):
                total = total + lower[i, m] * inverse[m, j]
            inverse[i, j] = -(scale[i] * total)
    index = lax.broadcasted_iota(jnp.int32, wide, 0)
    columns, rows = [], []
    for j in range(BASE):
        column = jnp.zeros(wide, jnp.float32)
        row = jnp.zeros(wide, jnp.float32)
        for i in range(j, BASE):
            column = jnp.where(index == i, inverse[i, j], column)
        for i in range(j + 1):
            row = jnp.where(index == i, inverse[j, i], row)
        columns.append(column)
        rows.append(row)
    return columns, rows


def combine(factors, panel):
    pieces = []
    for start in range(0, panel.shape[1], BLOCK):
        piece = panel[:, start : start + BLOCK]
        total = factors[0] * piece[0:1, :]
        for m in range(1, BASE):
            total = total + factors[m] * piece[m : m + 1, :]
        pieces.append(total)
    return jnp.concatenate(pieces, axis=1)


def ortho_kernel(gram_ref, left_ref, out_ref, rest, work, tail):
    rest[...] = gram_ref[...]
    tail[...] = left_ref[...]
    row = lax.broadcasted_iota(jnp.int32, (BLOCK, BLOCK), 0)
    column = lax.broadcasted_iota(jnp.int32, (BLOCK, BLOCK), 1)

    def block_step(k, carry):
        at = pl.ds(pl.multiple_of(k * BLOCK, BLOCK), BLOCK)
        work[:, :BLOCK] = rest[at, at]
        work[:, BLOCK:] = jnp.where(row == column, 1.0, 0.0).astype(jnp.float32)
        for first in range(0, BLOCK, BASE):
            panel = work[first : first + BASE, :]
            columns, rows = small_inverse(panel, first)
            solved = combine(columns, panel)
            work[first : first + BASE, :] = solved
            after = first + BASE
            if after < BLOCK:
                again = combine(rows, solved)
                parts = [again, jnp.zeros((BLOCK - after, 2 * BLOCK), jnp.float32)]
                if first:
                    parts = [jnp.zeros((first, 2 * BLOCK), jnp.float32)] + parts
                work[after:, :] = work[after:, :] - jnp.dot(
                    work[after:, :BLOCK], jnp.concatenate(parts, axis=0), precision=HIGHEST,
                    preferred_element_type=jnp.float32,
                )
        inverse = jnp.where(row >= column, work[:, BLOCK:], 0.0)
        panel = jnp.dot(inverse, rest[at, :], precision=HIGHEST, preferred_element_type=jnp.float32)
        lanes = lax.broadcasted_iota(jnp.int32, (BLOCK, RANK), 1)
        panel = jnp.where(lanes >= (k + 1) * BLOCK, panel, 0.0)
        rest[...] = rest[...] - lax.dot_general(
            panel, panel, (((0,), (0,)), ((), ())), precision=HIGHEST,
            preferred_element_type=jnp.float32,
        )
        done = lax.dot_general(
            tail[:, at], inverse, (((1,), (1,)), ((), ())), precision=HIGHEST,
            preferred_element_type=jnp.float32,
        )
        out_ref[:, at] = done.astype(out_ref.dtype)
        tail[...] = tail[...] - jnp.dot(
            done, panel, precision=HIGHEST, preferred_element_type=jnp.float32
        )
        return carry

    lax.fori_loop(0, RANK // BLOCK, block_step, 0)


def orthonormalize(gram, left):
    return pl.pallas_call(
        ortho_kernel,
        out_shape=jax.ShapeDtypeStruct(left.shape, jnp.bfloat16),
        in_specs=[VMEM, VMEM],
        out_specs=VMEM,
        scratch_shapes=[
            pltpu.VMEM((RANK, RANK), jnp.float32),
            pltpu.VMEM((BLOCK, 2 * BLOCK), jnp.float32),
            pltpu.VMEM(left.shape, jnp.float32),
        ],
        compiler_params=pltpu.CompilerParams(vmem_limit_bytes=48 * 2**20),
        name="orthonormalize",
    )(gram, left)


def right_kernel(
    wide_ref, ortho_ref, mine_ref, out_ref, chain, summed, landed,
    send1, recv1, send2, recv2, *gather_sems,
):
    y, z, _ = place()
    ring = (y, z)
    greet(plane_peers())

    def own(h, target, part):
        target = wrap(target)
        part = pl.ds(part * WIDTH, WIDTH)
        rows = pl.ds(h * HALF, HALF)
        block = wide_ref[target, part, rows] if h == 0 else wide_ref[part, target, rows]
        block = block.reshape(WIDTH * HALF, block.shape[-1])
        product = jnp.dot(block, ortho_ref[...], preferred_element_type=jnp.float32)
        return product.reshape(WIDTH, HALF, RANK)

    sends, arriving = [], {}

    def pass_on(h, d, p, step):
        copy = remote(
            chain.at[h, d, step - 1, p], chain.at[h, d, step, p],
            send1.at[h, d, step, p], recv1.at[h, d, step, p], line_device(h, 1 - 2 * d),
        )
        copy.start()
        sends.append(copy)
        arriving[h, d, p, step] = copy

    for h, d, p in CHAINS:
        length = chain_length(d, p)
        chain[h, d, 0, p] = own(h, ring[h] + (1 - 2 * d) * length, p).astype(jnp.bfloat16)
        pass_on(h, d, p, 1)
    for step in range(1, N // 2):
        for h, d, p in CHAINS:
            length = chain_length(d, p)
            if step < length:
                term = own(h, ring[h] + (1 - 2 * d) * (length - step), p)
                arriving[h, d, p, step].wait_recv()
                term = term + chain[h, d, step, p].astype(jnp.float32)
                chain[h, d, step, p] = term.astype(jnp.bfloat16)
                pass_on(h, d, p, step + 1)
    for h in range(2):
        for p in range(PARTS):
            term = own(h, ring[h], p)
            for d in range(2):
                length = chain_length(d, p)
                arriving[h, d, p, length].wait_recv()
                term = term + chain[h, d, length, p].astype(jnp.float32)
            summed[h, p * WIDTH : (p + 1) * WIDTH] = term
    second = {}
    for h in range(2):
        for k in range(1, N):
            copy = remote(
                summed.at[h, wrap(ring[1 - h] + k)], landed.at[h, k],
                send2.at[h, k], recv2.at[h, k], line_device(1 - h, k),
            )
            copy.start()
            sends.append(copy)
            second[h, k] = copy
    for h in range(2):
        total = summed[h, ring[1 - h]]
        for k in range(1, N):
            second[h, k].wait_recv()
            total = total + landed[h, k]
        mine_ref[pl.ds(h * HALF, HALF), :] = total.astype(jnp.bfloat16)
    gather_plane(mine_ref, out_ref, gather_sems)
    for copy in sends:
        copy.wait_send()


def sum_right(wide, ortho):
    return pl.pallas_call(
        right_kernel,
        out_shape=(
            jax.ShapeDtypeStruct((PAD, RANK), jnp.bfloat16),
            jax.ShapeDtypeStruct((N, N, PAD, RANK), jnp.bfloat16),
        ),
        in_specs=[VMEM, VMEM],
        out_specs=(VMEM, VMEM),
        scratch_shapes=[
            pltpu.VMEM((2, 2, N // 2 + 1, PARTS, WIDTH, HALF, RANK), jnp.bfloat16),
            pltpu.VMEM((2, N, HALF, RANK), jnp.float32),
            pltpu.VMEM((2, N, HALF, RANK), jnp.float32),
            pltpu.SemaphoreType.DMA((2, 2, N // 2 + 1, PARTS)),
            pltpu.SemaphoreType.DMA((2, 2, N // 2 + 1, PARTS)),
            pltpu.SemaphoreType.DMA((2, N)),
            pltpu.SemaphoreType.DMA((2, N)),
        ]
        + list(GATHER_SEMS),
        compiler_params=params(4),
        name="sum_right",
    )(wide, ortho)


def squares_kernel(x_ref, out_ref, landed, send, recv):
    tp = lax.axis_index("tp")
    greet([tp_device(k) for k in range(1, N)])
    copies = []
    for k in range(1, N):
        copy = remote(x_ref, landed.at[tp], send.at[k], recv.at[k], tp_device(k))
        copy.start()
        copies.append(copy)
    landed[tp] = x_ref[...]
    for copy in copies:
        copy.wait_recv()
    total = landed[0]
    for k in range(1, N):
        total = total + landed[k]
    out_ref[...] = total
    for copy in copies:
        copy.wait_send()


def sum_squares(x):
    return pl.pallas_call(
        squares_kernel,
        out_shape=jax.ShapeDtypeStruct(x.shape, jnp.float32),
        in_specs=[VMEM],
        out_specs=VMEM,
        scratch_shapes=[
            pltpu.VMEM((N,) + x.shape, jnp.float32),
            pltpu.SemaphoreType.DMA((N,)),
            pltpu.SemaphoreType.DMA((N,)),
        ],
        compiler_params=params(5),
        name="sum_squares",
    )(x)


def body(gradient, momentum, right_factor):
    whole = momentum + gradient.astype(jnp.float32)
    wide = whole.astype(jnp.bfloat16)
    row_count, columns = wide.shape
    blocks = wide.T.reshape(N * N, ROWS, row_count)
    blocks = jnp.pad(blocks, ((0, 0), (0, PAD - ROWS), (0, 0)))
    factor = gather(jnp.pad(right_factor, ((0, PAD - ROWS), (0, 0))))
    partial_value = lax.dot_general(
        blocks.reshape(N * N * PAD, row_count), factor.reshape(N * N * PAD, RANK),
        (((0,), (0,)), ((), ())), preferred_element_type=jnp.float32,
    )
    left = sum_left(partial_value)
    gram = spread_gram(sum_gram(jnp.dot(left.T, left, precision=HIGHEST)))
    ortho = orthonormalize(gram, left)
    mine, right = sum_right(blocks.reshape(N, N, PAD, row_count), ortho)
    right_f = right[:, :, :ROWS].reshape(columns, RANK).astype(jnp.float32)
    squares = jnp.sum((right_f * right_f).reshape(columns // N, N, RANK), axis=0)
    squares = jnp.sum(sum_squares(squares), axis=0)
    norms = jnp.sqrt(squares + 1e-06)
    factor_new = (math.sqrt(FFW) * mine[:ROWS].astype(jnp.float32) / norms).astype(jnp.bfloat16)
    factor_all = (math.sqrt(FFW) * right_f / norms).astype(jnp.bfloat16)
    scaled = (ortho.astype(jnp.float32) * (norms / math.sqrt(FFW))).astype(jnp.bfloat16)
    combined = lax.dot_general(
        jnp.concatenate([ortho, scaled], axis=0), factor_all,
        (((1,), (1,)), ((), ())), preferred_element_type=jnp.float32,
    )
    update = (math.sqrt(D / RANK) * combined[:row_count]).astype(jnp.bfloat16)
    momentum_new = whole - 0.05 * combined[row_count:]
    return (update, momentum_new, factor_new)


def solution(mesh):
    return jax.shard_map(
        body,
        mesh=mesh,
        in_specs=(P("fsdp", "tp"), P("fsdp", "tp"), P(("tp", "fsdp"), None)),
        out_specs=(P("fsdp", "tp"), P("fsdp", "tp"), P(("tp", "fsdp"), None)),
        check_vma=False,
    )
```

time: 782 us -> 214 us (0.27)
  waiting for transfers between devices: 397 us -> 0 us
  Pallas kernels: 0 us -> 186 us
  blocking collectives: 172 us -> 0 us
  other arithmetic: 122 us -> 9.98 us
  starting transfers between devices: 33.4 us -> 0 us
  between operations: 17.4 us -> 0.76 us
  matrix products: 18.5 us -> 4.32 us
  local copies, waits for them, and re-layouts: 21.1 us -> 10.7 us
    psum x2 -> x0, waiting for transfers between devices: 227 us -> none  [the longest x1 162 us: body(): lax.psum(jnp.dot(left.T, left, precision=lax.Precision.HIGHEST), 'fsdp')]
    pallas_call x0 -> x7, Pallas kernels: none -> 186 us  [the longest x1 58.6 us: sum_right(): pl.pallas_call(right_kernel, out_shape=(jax.ShapeDtypeStruct((PAD, RANK),...]
    all_gather x2 -> x0, waiting for transfers between devices: 169 us -> none  [the longest x1 91.4 us: body(): lax.all_gather(right_factor, 'fsdp', axis=0, tiled=True)]
    another operation x17 -> x0, other arithmetic: 119 us -> none  [the longest x14 78.6 us: body(): lower = jnp.linalg.cholesky(gram)]
    psum x1 -> x0, blocking collectives: 94.9 us -> none  [body(): norms = jnp.sqrt(lax.psum(squares, ('fsdp', 'tp')) + 1e-06)]
    unnamed x1 -> x0, blocking collectives: 76.8 us -> none
    unnamed x8 -> x0, starting transfers between devices: 33.2 us -> none
    another operation x13 -> x0, matrix products: 11.1 us -> none  [the longest x7 5.67 us: body(): jax.scipy.linalg.solve_triangular(lower, left.T, lower=True)]
  transfers between devices with their start and end apart: 12 -> 0, of which waited for: 4 -> 0; matrix products, arithmetic and copies ran while one was open for 0% -> 0% of each run, Pallas kernels for 0% -> 0%
where the time goes in v1:
time: 214 us; the launch traced here: 211 us
  Pallas kernels  186 us (87%)
  local copies, waits for them, and re-layouts  10.7 us (5%)
  other arithmetic  9.98 us (5%)
  matrix products  4.32 us (2%)
    pallas_call x1, Pallas kernels, sum_right(): pl.pallas_call(right_kernel, out_shape=(jax.ShapeDtypeStruct((PAD, RANK),...  58.6 us
    pallas_call x1, Pallas kernels, gather(): pl.pallas_call(gather_kernel, out_shape=jax.ShapeDtypeStruct((N, N, PAD,...  37.9 us
    pallas_call x1, Pallas kernels, orthonormalize(): pl.pallas_call(ortho_kernel, out_shape=jax.ShapeDtypeStruct(left.shape, j...  35.6 us
    pallas_call x1, Pallas kernels, sum_gram(): pl.pallas_call(gram_kernel, out_shape=jax.ShapeDtypeStruct((RANK // N, RA...  23.5 us
    pallas_call x1, Pallas kernels, sum_left(): pl.pallas_call(left_kernel, out_shape=jax.ShapeDtypeStruct(partial_value....  11.8 us
    pallas_call x1, Pallas kernels, spread_gram(): pl.pallas_call(spread_kernel, out_shape=jax.ShapeDtypeStruct((RANK, RANK)...  11.6 us
    pallas_call x1, Pallas kernels, sum_squares(): pl.pallas_call(squares_kernel, out_shape=jax.ShapeDtypeStruct(x.shape, jn...  6.59 us
    mul x1, local copies, waits for them, and re-layouts, body(): right_f * right_f  4.75 us

profile of v1, /device:TPU:6, one launch (start us, length us, event | category | flops | bytes accessed | tf_op | source)
XLA Modules:
  0.0 211.3 jit_solution(7315576212994246420)
XLA Ops:
  0.6 0.8 pad.9.x_ref
  1.4 1.4 fusion.4
  2.8 0.3 copy.7
  3.0 0.1 reshape.33
  3.1 0.1 pad.8
  3.2 37.9 %gather_factor.1 = bf16[8,8,32,512]{3,2,1,0:T(8,128)(2,1)S(1)} custom-call(bf16[32,512]{1,0:T(8,128)(2,1)S(1)} %pad.9.x_ref), custom_call_target="tpu_custom_call" | custom-call | tf_op jit(solution)/shard_map/gather_factor/pallas_call | solution.py:128
  41.1 0.5 fusion.9.x_ref
  41.6 11.8 %sum_left.1.left_ref = f32[128,512]{1,0:T(8,128)S(1)} custom-call(f32[128,512]{1,0:T(8,128)S(1)} %fusion.9.x_ref), custom_call_target="tpu_custom_call" | custom-call | tf_op jit(solution)/shard_map/sum_left/pallas_call | solution.py:176
  53.4 1.0 fusion.10.gram_ref
  54.4 23.5 %sum_gram.1.x_ref = f32[64,512]{1,0:T(8,128)S(1)} custom-call(f32[512,512]{1,0:T(8,128)S(1)} %fusion.10.gram_ref), custom_call_target="tpu_custom_call" | custom-call | tf_op jit(solution)/shard_map/sum_gram/pallas_call | solution.py:229
  77.9 11.6 %spread_gram.1.gram_ref = f32[512,512]{1,0:T(8,128)S(1)} custom-call(f32[64,512]{1,0:T(8,128)S(1)} %sum_gram.1.x_ref), custom_call_target="tpu_custom_call" | custom-call | tf_op jit(solution)/shard_map/spread_gram/pallas_call | solution.py:278
  89.5 35.6 %orthonormalize.1.ortho_ref = bf16[128,512]{1,0:T(8,128)(2,1)S(1)} custom-call(f32[512,512]{1,0:T(8,128)S(1)} %spread_gram.1.gram_ref, f32[128,512]{1,0:T(8,128)S(1)} %sum_left.1.left_ref), custom_call_target="tpu_custom_call" | custom-call | tf_op jit(solution)/shard_map/orthonormalize/pallas_call | solution.py:389
  125.1 58.6 %sum_right.1 = (bf16[32,512]{1,0:T(8,128)(2,1)S(1)}, bf16[8,8,32,512]{3,2,1,0:T(8,128)(2,1)S(1)}) custom-call(bf16[8,8,32,128]{3,2,1,0:T(8,128)(2,1)S(1)} %bitcast.11, bf16[128,512]{1,0:T(8,128)(2,1)S(1)} %orthonormalize.1.ortho_ref), custom_call_target="tpu_custom_call" | custom-call | tf_op jit(solution)/shard_map/sum_right/pallas_call | solution.py:475
  183.7 4.3 %convert_multiply_fusion.1 = (f32[8,8,28,512]{3,2,1,0:T(8,128)}, f32[8,8,28,512]{3,2,1,0:T(8,128)}) fusion(bf16[8,8,32,512]{3,2,1,0:T(8,128)(2,1)S(1)} %get-tuple-element.5), kind=kLoop, calls=%fused_computation.1 | loop fusion | flops 2752512 | bytes 9175040 | tf_op jit(solution)/shard_map/mul | solution.py:549
  188.1 4.7 %mul.43 = f32[224,8,512]{2,1,0:T(8,128)} reshape(f32[8,8,28,512]{3,2,1,0:T(8,128)} %get-tuple-element.7) | data formatting | bytes 7340032 | tf_op jit(solution)/shard_map/mul | solution.py:549
  192.8 2.3 %reduce_sum.18.x_ref = f32[8,512]{1,0:T(8,128)S(1)} reduce(f32[224,8,512]{2,1,0:T(8,128)} %mul.43, f32[]{:T(128)} %constant.2.clone.1), dimensions={0}, to_apply=%region_0.1 | reduce | flops 913408 | bytes 3686404 | tf_op jit(solution)/shard_map/reduce_sum | solution.py:549
  195.2 6.6 %sum_squares.1 = f32[8,512]{1,0:T(8,128)S(1)} custom-call(f32[8,512]{1,0:T(8,128)S(1)} %reduce_sum.18.x_ref), custom_call_target="tpu_custom_call" | custom-call | tf_op jit(solution)/shard_map/sum_squares/pallas_call | solution.py:518
  201.8 0.6 divide_convert_fusion.2
  202.4 4.7 %mul.48 = f32[1792,512]{1,0:T(8,128)} reshape(f32[8,8,28,512]{3,2,1,0:T(8,128)} %get-tuple-element.8) | data formatting | bytes 7340032 | tf_op jit(solution)/shard_map/mul | solution.py:553
  207.2 0.0 copy-start
  207.2 2.8 %fusion = f32[256,1792]{1,0:T(8,128)S(1)} fusion(f32[1792,512]{1,0:T(8,128)} %mul.48, f32[512]{0:T(512)S(1)} %get-tuple-element.12, bf16[128,512]{1,0:T(8,128)(2,1)S(1)} %multiply_convert_fusion, bf16[128,512]{1,0:T(8,128)(2,1)S(1)} %orthonormalize.1.ortho_ref), kind=kOutput, calls=%fused_computation.3 | convolution fusion | flops 472121344 | bytes 5769216 | tf_op jit(solution)/shard_map/dot_general | solution.py:555
  210.0 0.0 copy-done
  210.0 0.0 copy-done.1
  210.0 1.3 fusion.1
  (4 shorter events, 0.1 us)
Async XLA Ops:
  207.2 2.8 %copy-start = (f32[128,1792]{1,0:T(8,128)S(1)}, f32[128,1792]{1,0:T(8,128)}, u32[]{:S(2)}) copy-start(f32[128,1792]{1,0:T(8,128)} %param.4) | copy-start | bytes 2752516
  207.2 2.8 %copy-start.1 = (bf16[128,1792]{1,0:T(8,128)(2,1)S(1)}, bf16[128,1792]{1,0:T(8,128)(2,1)}, u32[]{:S(2)}) copy-start(bf16[128,1792]{1,0:T(8,128)(2,1)} %param.3) | copy-start | bytes 1376260

commit v2 on v1

--- a/solution.py
+++ b/solution.py
@@ -66,10 +66,10 @@
     return N // 2 if direction == part else N // 2 - 1
 
 
-CHAINS = [(h, d, p) for h in range(2) for d in range(2) for p in range(PARTS)]
-
-
-def gather_plane(x_ref, out_ref, sems):
+CHAINS = [(h, d, p) for p in range(PARTS) for h in range(2) for d in range(2)]
+
+
+def gather_plane(x_ref, out_ref, sems, visit=None):
     send1, recv1, send2, recv2 = sems
     y, z, _ = place()
     ring = (y, z)
@@ -107,6 +107,10 @@
                 copy.start()
                 sends.append(copy)
                 arriving[h, d, p, step] = copy
+        if visit is not None:
+            for h, d, p in CHAINS:
+                if step <= chain_length(d, p) + 1 and (step > 1 or d == 0):
+                    visit(slot(h, wrap(ring[h] - (1 - 2 * d) * (step - 1)), p))
     for copy in sends:
         copy.wait_send()
 
@@ -328,61 +332,84 @@
     return columns, rows
 
 
+def add_up(terms):
+    while len(terms) > 1:
+        terms = [sum(terms[i + 1 : i + 2], terms[i]) for i in range(0, len(terms), 2)]
+    return terms[0]
+
+
 def combine(factors, panel):
-    pieces = []
-    for start in range(0, panel.shape[1], BLOCK):
-        piece = panel[:, start : start + BLOCK]
-        total = factors[0] * piece[0:1, :]
-        for m in range(1, BASE):
-            total = total + factors[m] * piece[m : m + 1, :]
-        pieces.append(total)
-    return jnp.concatenate(pieces, axis=1)
-
-
-def ortho_kernel(gram_ref, left_ref, out_ref, rest, work, tail):
+    return [
+        add_up([factors[m] * piece[m : m + 1, :] for m in range(BASE)]) for piece in panel
+    ]
+
+
+def block_inverse(block):
+    row = lax.broadcasted_iota(jnp.int32, (BLOCK, BLOCK), 0)
+    column = lax.broadcasted_iota(jnp.int32, (BLOCK, BLOCK), 1)
+    unit = jnp.where(row == column, 1.0, 0.0).astype(jnp.float32)
+    count = BLOCK // BASE
+    panels = [
+        [matrix[b * BASE : (b + 1) * BASE, :] for matrix in (block, unit)] for b in range(count)
+    ]
+    solved = []
+    for b in range(count):
+        first = b * BASE
+        columns, rows = small_inverse(panels[b][0], first)
+        done = combine(columns, panels[b])
+        solved.append(done[1])
+        if b + 1 == count:
+            break
+        again = combine(rows, done)
+        ahead = panels[b + 1]
+        factors = [
+            jnp.broadcast_to(ahead[0][:, first + m : first + m + 1], (BASE, BLOCK))
+            for m in range(BASE)
+        ]
+        panels[b + 1] = [old - new for old, new in zip(ahead, combine(factors, again))]
+        if b + 2 == count:
+            continue
+        multiplier = jnp.concatenate([panels[c][0] for c in range(b + 2, count)], axis=0)
+        parts = [jnp.concatenate(again, axis=1)]
+        parts.append(jnp.zeros((BLOCK - first - BASE, 2 * BLOCK), jnp.float32))
+        if first:
+            parts.insert(0, jnp.zeros((first, 2 * BLOCK), jnp.float32))
+        change = jnp.dot(
+            multiplier, jnp.concatenate(parts, axis=0), precision=HIGHEST,
+            preferred_element_type=jnp.float32,
+        )
+        for c in range(b + 2, count):
+            at = (c - b - 2) * BASE
+            panels[c] = [
+                old - change[at : at + BASE, i * BLOCK : (i + 1) * BLOCK]
+                for i, old in enumerate(panels[c])
+            ]
+    return jnp.where(row >= column, jnp.concatenate(solved, axis=0), 0.0)
+
+
+def full_dot(x, y, dims):
+    return lax.dot_general(
+        x, y, (dims, ((), ())), precision=HIGHEST, preferred_element_type=jnp.float32
+    )
+
+
+def ortho_kernel(gram_ref, left_ref, out_ref, rest, tail):
     rest[...] = gram_ref[...]
     tail[...] = left_ref[...]
-    row = lax.broadcasted_iota(jnp.int32, (BLOCK, BLOCK), 0)
-    column = lax.broadcasted_iota(jnp.int32, (BLOCK, BLOCK), 1)
-
-    def block_step(k, carry):
-        at = pl.ds(pl.multiple_of(k * BLOCK, BLOCK), BLOCK)
-        work[:, :BLOCK] = rest[at, at]
-        work[:, BLOCK:] = jnp.where(row == column, 1.0, 0.0).astype(jnp.float32)
-        for first in range(0, BLOCK, BASE):
-            panel = work[first : first + BASE, :]
-            columns, rows = small_inverse(panel, first)
-            solved = combine(columns, panel)
-            work[first : first + BASE, :] = solved
-            after = first + BASE
-            if after < BLOCK:
-                again = combine(rows, solved)
-                parts = [again, jnp.zeros((BLOCK - after, 2 * BLOCK), jnp.float32)]
-                if first:
-                    parts = [jnp.zeros((first, 2 * BLOCK), jnp.float32)] + parts
-                work[after:, :] = work[after:, :] - jnp.dot(
-                    work[after:, :BLOCK], jnp.concatenate(parts, axis=0), precision=HIGHEST,
-                    preferred_element_type=jnp.float32,
-                )
-        inverse = jnp.where(row >= column, work[:, BLOCK:], 0.0)
-        panel = jnp.dot(inverse, rest[at, :], precision=HIGHEST, preferred_element_type=jnp.float32)
-        lanes = lax.broadcasted_iota(jnp.int32, (BLOCK, RANK), 1)
-        panel = jnp.where(lanes >= (k + 1) * BLOCK, panel, 0.0)
-        rest[...] = rest[...] - lax.dot_general(
-            panel, panel, (((0,), (0,)), ((), ())), precision=HIGHEST,
-            preferred_element_type=jnp.float32,
-        )
-        done = lax.dot_general(
-            tail[:, at], inverse, (((1,), (1,)), ((), ())), precision=HIGHEST,
-            preferred_element_type=jnp.float32,
-        )
-        out_ref[:, at] = done.astype(out_ref.dtype)
-        tail[...] = tail[...] - jnp.dot(
-            done, panel, precision=HIGHEST, preferred_element_type=jnp.float32
-        )
-        return carry
-
-    lax.fori_loop(0, RANK // BLOCK, block_step, 0)
+    for at in range(0, RANK, BLOCK):
+        end = at + BLOCK
+        inverse = block_inverse(rest[at:end, at:end])
+        done = full_dot(tail[:, at:end], inverse, ((1,), (1,)))
+        out_ref[:, at:end] = done.astype(out_ref.dtype)
+        if end == RANK:
+            break
+        panel = full_dot(inverse, rest[at:end, end:], ((1,), (0,)))
+        for start in range(end, RANK, BLOCK):
+            piece = panel[:, start - end : start - end + BLOCK]
+            rest[start : start + BLOCK, start:] -= full_dot(
+                piece, panel[:, start - end :], ((0,), (0,))
+            )
+        tail[:, end:] -= full_dot(done, panel, ((1,), (0,)))
 
 
 def orthonormalize(gram, left):
@@ -393,7 +420,6 @@
         out_specs=VMEM,
         scratch_shapes=[
             pltpu.VMEM((RANK, RANK), jnp.float32),
-            pltpu.VMEM((BLOCK, 2 * BLOCK), jnp.float32),
             pltpu.VMEM(left.shape, jnp.float32),
         ],
         compiler_params=pltpu.CompilerParams(vmem_limit_bytes=48 * 2**20),
@@ -402,7 +428,7 @@
 
 
 def right_kernel(
-    wide_ref, ortho_ref, mine_ref, out_ref, chain, summed, landed,
+    wide_ref, ortho_ref, mine_ref, out_ref, squares_ref, chain, summed, landed,
     send1, recv1, send2, recv2, *gather_sems,
 ):
     y, z, _ = place()
@@ -449,7 +475,7 @@
                 length = chain_length(d, p)
                 arriving[h, d, p, length].wait_recv()
                 term = term + chain[h, d, length, p].astype(jnp.float32)
-            summed[h, p * WIDTH : (p + 1) * WIDTH] = term
+            summed[h, p * WIDTH : (p + 1) * WIDTH] = term.astype(jnp.bfloat16)
     second = {}
     for h in range(2):
         for k in range(1, N):
@@ -461,12 +487,18 @@
             sends.append(copy)
             second[h, k] = copy
     for h in range(2):
-        total = summed[h, ring[1 - h]]
+        total = summed[h, ring[1 - h]].astype(jnp.float32)
         for k in range(1, N):
             second[h, k].wait_recv()
-            total = total + landed[h, k]
+            total = total + landed[h, k].astype(jnp.float32)
         mine_ref[pl.ds(h * HALF, HALF), :] = total.astype(jnp.bfloat16)
-    gather_plane(mine_ref, out_ref, gather_sems)
+    squares_ref[...] = jnp.zeros_like(squares_ref)
+
+    def add_squares(ref):
+        block = ref[...].astype(jnp.float32).reshape(WIDTH * HALF // N, N, RANK)
+        squares_ref[...] += jnp.sum(block * block, axis=0)
+
+    gather_plane(mine_ref, out_ref, gather_sems, add_squares)
     for copy in sends:
         copy.wait_send()
 
@@ -477,13 +509,14 @@
         out_shape=(
             jax.ShapeDtypeStruct((PAD, RANK), jnp.bfloat16),
             jax.ShapeDtypeStruct((N, N, PAD, RANK), jnp.bfloat16),
+            jax.ShapeDtypeStruct((N, RANK), jnp.float32),
         ),
         in_specs=[VMEM, VMEM],
-        out_specs=(VMEM, VMEM),
+        out_specs=(VMEM, VMEM, VMEM),
         scratch_shapes=[
             pltpu.VMEM((2, 2, N // 2 + 1, PARTS, WIDTH, HALF, RANK), jnp.bfloat16),
-            pltpu.VMEM((2, N, HALF, RANK), jnp.float32),
-            pltpu.VMEM((2, N, HALF, RANK), jnp.float32),
+            pltpu.VMEM((2, N, HALF, RANK), jnp.bfloat16),
+            pltpu.VMEM((2, N, HALF, RANK), jnp.bfloat16),
             pltpu.SemaphoreType.DMA((2, 2, N // 2 + 1, PARTS)),
             pltpu.SemaphoreType.DMA((2, 2, N // 2 + 1, PARTS)),
             pltpu.SemaphoreType.DMA((2, N)),
@@ -530,10 +563,66 @@
     )(x)
 
 
+def finish_kernel(
+    squares_ref, right_ref, mine_ref, ortho_ref, gradient_ref, momentum_ref,
+    update_ref, new_ref, factor_ref, factor,
+):
+    squares = jnp.sum(squares_ref[...], axis=0, keepdims=True)
+    norms = jnp.sqrt(squares + 1e-06)
+    gain = math.sqrt(FFW) / norms
+    factor_ref[...] = (mine_ref[...].astype(jnp.float32) * gain)[:ROWS].astype(jnp.bfloat16)
+    ortho = ortho_ref[...]
+    scaled = (ortho.astype(jnp.float32) * (norms / math.sqrt(FFW))).astype(jnp.bfloat16)
+    stacked = jnp.concatenate([ortho, scaled], axis=0)
+    group = 4
+    for first in range(0, right_ref.shape[0], group):
+        pieces = [
+            (right_ref[first + i].astype(jnp.float32) * gain)[:ROWS] for i in range(group)
+        ]
+        factor[first * ROWS : (first + group) * ROWS, :] = jnp.concatenate(
+            pieces, axis=0
+        ).astype(jnp.bfloat16)
+    combined = lax.dot_general(
+        stacked, factor[...], (((1,), (1,)), ((), ())), preferred_element_type=jnp.float32
+    )
+    rows = ortho.shape[0]
+    update_ref[...] = (math.sqrt(D / RANK) * combined[:rows]).astype(jnp.bfloat16)
+    whole = momentum_ref[...] + gradient_ref[...].astype(jnp.float32)
+    new_ref[...] = whole - 0.05 * combined[rows:]
+
+
+def finish(squares, right, mine, ortho, gradient, momentum):
+    steps = 2
+    rows, columns = gradient.shape
+    blocks = N * N // steps
+    whole = lambda shape: pl.BlockSpec(shape, lambda i: (0, 0))
+    tile = pl.BlockSpec((rows, columns // steps), lambda i: (0, i))
+    return pl.pallas_call(
+        finish_kernel,
+        grid=(steps,),
+        out_shape=(
+            jax.ShapeDtypeStruct((rows, columns), jnp.bfloat16),
+            jax.ShapeDtypeStruct((rows, columns), jnp.float32),
+            jax.ShapeDtypeStruct((ROWS, RANK), jnp.bfloat16),
+        ),
+        in_specs=[
+            whole((N, RANK)),
+            pl.BlockSpec((blocks, PAD, RANK), lambda i: (i, 0, 0)),
+            whole((PAD, RANK)),
+            whole((rows, RANK)),
+            tile,
+            tile,
+        ],
+        out_specs=(tile, tile, whole((ROWS, RANK))),
+        scratch_shapes=[pltpu.VMEM((blocks * ROWS, RANK), jnp.bfloat16)],
+        compiler_params=pltpu.CompilerParams(vmem_limit_bytes=48 * 2**20),
+        name="finish",
+    )(squares, right, mine, ortho, gradient, momentum)
+
+
 def body(gradient, momentum, right_factor):
-    whole = momentum + gradient.astype(jnp.float32)
-    wide = whole.astype(jnp.bfloat16)
-    row_count, columns = wide.shape
+    wide = (momentum + gradient.astype(jnp.float32)).astype(jnp.bfloat16)
+    row_count = wide.shape[0]
     blocks = wide.T.reshape(N * N, ROWS, row_count)
     blocks = jnp.pad(blocks, ((0, 0), (0, PAD - ROWS), (0, 0)))
     factor = gather(jnp.pad(right_factor, ((0, PAD - ROWS), (0, 0))))
@@ -544,21 +633,9 @@
     left = sum_left(partial_value)
     gram = spread_gram(sum_gram(jnp.dot(left.T, left, precision=HIGHEST)))
     ortho = orthonormalize(gram, left)
-    mine, right = sum_right(blocks.reshape(N, N, PAD, row_count), ortho)
-    right_f = right[:, :, :ROWS].reshape(columns, RANK).astype(jnp.float32)
-    squares = jnp.sum((right_f * right_f).reshape(columns // N, N, RANK), axis=0)
-    squares = jnp.sum(sum_squares(squares), axis=0)
-    norms = jnp.sqrt(squares + 1e-06)
-    factor_new = (math.sqrt(FFW) * mine[:ROWS].astype(jnp.float32) / norms).astype(jnp.bfloat16)
-    factor_all = (math.sqrt(FFW) * right_f / norms).astype(jnp.bfloat16)
-    scaled = (ortho.astype(jnp.float32) * (norms / math.sqrt(FFW))).astype(jnp.bfloat16)
-    combined = lax.dot_general(
-        jnp.concatenate([ortho, scaled], axis=0), factor_all,
-        (((1,), (1,)), ((), ())), preferred_element_type=jnp.float32,
-    )
-    update = (math.sqrt(D / RANK) * combined[:row_count]).astype(jnp.bfloat16)
-    momentum_new = whole - 0.05 * combined[row_count:]
-    return (update, momentum_new, factor_new)
+    mine, right, squares = sum_right(blocks.reshape(N, N, PAD, row_count), ortho)
+    right = right.reshape(N * N, PAD, RANK)
+    return finish(sum_squares(squares), right, mine, ortho, gradient, momentum)
 
 
 def solution(mesh):

time: 214 us -> 173 us (0.81)
  Pallas kernels: 186 us -> 166 us
  local copies, waits for them, and re-layouts: 10.7 us -> 1.19 us
  other arithmetic: 9.98 us -> 1.37 us
  matrix products: 4.32 us -> 1.5 us
    pallas_call x1, Pallas kernels: 35.6 us -> 19.8 us  [orthonormalize(): pl.pallas_call(ortho_kernel, out_shape=jax.ShapeDtypeStruct(left.shape, j...]
    mul x2 -> x0, local copies, waits for them, and re-layouts: 9.49 us -> none  [the longest x1 4.75 us: body(): right_f * right_f]
    mul x1 -> x0, other arithmetic: 4.35 us -> none  [body(): right_f * right_f]
    pallas_call x1, Pallas kernels: 58.6 us -> 55.1 us  [sum_right(): pl.pallas_call(right_kernel, out_shape=(jax.ShapeDtypeStruct((PAD, RANK),...]
    dot_general x1 -> x0, matrix products: 2.83 us -> none  [body(): lax.dot_general(jnp.concatenate([ortho, scaled], axis=0), factor_all, (((...]
    reduce_sum x2 -> x0, other arithmetic: 2.34 us -> none  [the longest x1 2.32 us: body(): jnp.sum((right_f * right_f).reshape(columns // N, N, RANK), axis=0)]
    pallas_call x0 -> x1, Pallas kernels: none -> 2.18 us  [finish(): pl.pallas_call(finish_kernel, grid=(steps,), out_shape=(jax.ShapeDtypeStr...]
where the time goes in v2:
time: 173 us; the launch traced here: 171 us
  Pallas kernels  166 us (96%)
    pallas_call x1, Pallas kernels, sum_right(): pl.pallas_call(right_kernel, out_shape=(jax.ShapeDtypeStruct((PAD, RANK),...  55.1 us
    pallas_call x1, Pallas kernels, gather(): pl.pallas_call(gather_kernel, out_shape=jax.ShapeDtypeStruct((N, N, PAD,...  36.9 us
    pallas_call x1, Pallas kernels, sum_gram(): pl.pallas_call(gram_kernel, out_shape=jax.ShapeDtypeStruct((RANK // N, RA...  22.3 us
    pallas_call x1, Pallas kernels, orthonormalize(): pl.pallas_call(ortho_kernel, out_shape=jax.ShapeDtypeStruct(left.shape, j...  19.8 us
    pallas_call x1, Pallas kernels, sum_left(): pl.pallas_call(left_kernel, out_shape=jax.ShapeDtypeStruct(partial_value....  11.8 us
    pallas_call x1, Pallas kernels, spread_gram(): pl.pallas_call(spread_kernel, out_shape=jax.ShapeDtypeStruct((RANK, RANK)...  11.3 us
    pallas_call x1, Pallas kernels, sum_squares(): pl.pallas_call(squares_kernel, out_shape=jax.ShapeDtypeStruct(x.shape, jn...  6.61 us

profile of v2, /device:TPU:6, one launch (start us, length us, event | category | flops | bytes accessed | tf_op | source)
XLA Modules:
  0.0 170.8 jit_solution(18249149645305773249)
XLA Ops:
  0.6 0.8 pad.9.x_ref
  1.4 1.4 fusion
  2.8 0.3 copy.7
  3.0 0.1 reshape.21
  3.1 0.1 pad.8
  3.2 36.9 %gather_factor.1 = bf16[8,8,32,512]{3,2,1,0:T(8,128)(2,1)S(1)} custom-call(bf16[32,512]{1,0:T(8,128)(2,1)S(1)} %pad.9.x_ref), custom_call_target="tpu_custom_call" | custom-call | tf_op jit(solution)/shard_map/gather_factor/pallas_call | solution.py:132
  40.1 0.5 fusion.1.x_ref
  40.6 11.8 %sum_left.1.left_ref = f32[128,512]{1,0:T(8,128)S(1)} custom-call(f32[128,512]{1,0:T(8,128)S(1)} %fusion.1.x_ref), custom_call_target="tpu_custom_call" | custom-call | tf_op jit(solution)/shard_map/sum_left/pallas_call | solution.py:180
  52.4 1.0 fusion.2.gram_ref
  53.4 0.0 copy-start
  53.4 0.0 copy-start.1
  53.5 22.3 %sum_gram.1.x_ref = f32[64,512]{1,0:T(8,128)S(1)} custom-call(f32[512,512]{1,0:T(8,128)S(1)} %fusion.2.gram_ref), custom_call_target="tpu_custom_call" | custom-call | tf_op jit(solution)/shard_map/sum_gram/pallas_call | solution.py:233
  75.8 11.3 %spread_gram.1.gram_ref = f32[512,512]{1,0:T(8,128)S(1)} custom-call(f32[64,512]{1,0:T(8,128)S(1)} %sum_gram.1.x_ref), custom_call_target="tpu_custom_call" | custom-call | tf_op jit(solution)/shard_map/spread_gram/pallas_call | solution.py:282
  87.1 19.8 %orthonormalize.1.ortho_ref = bf16[128,512]{1,0:T(8,128)(2,1)S(1)} custom-call(f32[512,512]{1,0:T(8,128)S(1)} %spread_gram.1.gram_ref, f32[128,512]{1,0:T(8,128)S(1)} %sum_left.1.left_ref), custom_call_target="tpu_custom_call" | custom-call | tf_op jit(solution)/shard_map/orthonormalize/pallas_call | solution.py:416
  106.9 55.1 %sum_right.1 = (bf16[32,512]{1,0:T(8,128)(2,1)S(1)}, bf16[8,8,32,512]{3,2,1,0:T(8,128)(2,1)S(1)}, f32[8,512]{1,0:T(8,128)S(1)}) custom-call(bf16[8,8,32,128]{3,2,1,0:T(8,128)(2,1)S(1)} %bitcast.12, bf16[128,512]{1,0:T(8,128)(2,1)S(1)} %orthonormalize.1.ortho_ref), custom_call_target="tpu_custom_call" | custom-call | tf_op jit(solution)/shard_map/sum_right/pallas_call | solution.py:507
  162.0 6.6 %sum_squares.1.squares_ref = f32[8,512]{1,0:T(8,128)S(1)} custom-call(f32[8,512]{1,0:T(8,128)S(1)} %get-tuple-element.6.x_ref), custom_call_target="tpu_custom_call" | custom-call | tf_op jit(solution)/shard_map/sum_squares/pallas_call | solution.py:551
  168.6 0.0 copy-done
  168.6 0.0 copy-done.1
  168.6 2.2 %finish.1 = (bf16[128,1792]{1,0:T(8,128)(2,1)}, f32[128,1792]{1,0:T(8,128)}, bf16[28,512]{1,0:T(8,128)(2,1)}) custom-call(f32[8,512]{1,0:T(8,128)S(1)} %sum_squares.1.squares_ref, bf16[64,32,512]{2,1,0:T(8,128)(2,1)S(1)} %bitcast.13, bf16[32,512]{1,0:T(8,128)(2,1)S(1)} %get-tuple-element.8.mine_ref, bf16[128,512]{1,0:T(8,128)(2,1)S(1)} %orthonormalize.1.ortho_ref, ...), custom_call_target="tpu_custom_call" | custom-call | tf_op jit(solution)/shard_map/finish/pallas_call | solution.py:600
Async XLA Ops:
  53.4 115.2 %copy-start = (f32[128,1792]{1,0:T(8,128)S(1)}, f32[128,1792]{1,0:T(8,128)}, u32[]{:S(2)}) copy-start(f32[128,1792]{1,0:T(8,128)} %momentum_ref.1) | copy-start | bytes 2752516
  53.4 115.2 %copy-start.1 = (bf16[128,1792]{1,0:T(8,128)(2,1)S(1)}, bf16[128,1792]{1,0:T(8,128)(2,1)}, u32[]{:S(2)}) copy-start(bf16[128,1792]{1,0:T(8,128)(2,1)} %gradient_ref.1) | copy-start | bytes 1376260

commit v3 on v0

v3 whole, which is shorter than its diff:
```python
import functools
import math

import jax
import jax.numpy as jnp
from jax import lax
from jax.experimental import pallas as pl
from jax.experimental.pallas import tpu as pltpu
from jax.sharding import PartitionSpec as P

D = 8192
FFW = 14336
RANK = 512
N = 8
ROWS = 28
PAD = 32
HALF = 16
PARTS = 2
WIDTH = N // PARTS
MESH = pl.DeviceIdType.MESH
HIGHEST = lax.Precision.HIGHEST
VMEM = pl.BlockSpec(memory_space=pltpu.VMEM)


def params(collective_id):
    return pltpu.CompilerParams(
        collective_id=collective_id, has_side_effects=True, vmem_limit_bytes=48 * 2**20
    )


def wrap(index):
    return lax.rem(index + 2 * N, N)


def greet(peers):
    barrier = pltpu.get_barrier_semaphore()
    for peer in peers:
        pl.semaphore_signal(barrier, inc=1, device_id=peer, device_id_type=MESH)
    pl.semaphore_wait(barrier, len(peers))


def remote(src, dst, send_sem, recv_sem, device):
    return pltpu.make_async_remote_copy(
        src_ref=src, dst_ref=dst, send_sem=send_sem, recv_sem=recv_sem,
        device_id=device, device_id_type=MESH,
    )


def place():
    fsdp = lax.axis_index("fsdp")
    return fsdp // N, lax.rem(fsdp, N), lax.axis_index("tp")


def line_device(axis, offset):
    y, z, tp = place()
    if axis == 0:
        return (wrap(y + offset) * N + z, tp)
    return (y * N + wrap(z + offset), tp)


def tp_device(offset):
    return (lax.axis_index("fsdp"), wrap(lax.axis_index("tp") + offset))


def all_peers():
    plane = [line_device(axis, k) for axis in range(2) for k in range(1, N)]
    return plane + [tp_device(k) for k in range(1, N)]


def chain_length(direction, part):
    return N // 2 if direction == part else N // 2 - 1


CHAINS = [(h, d, p) for p in range(PARTS) for h in range(2) for d in range(2)]
CHAIN_SEMS = (2, 2, N // 2, PARTS)


def gather_plane(mine, out, sems, visit, sends):
    send1, recv1, send2, recv2 = sems
    y, z, _ = place()
    ring, across = (y, z), (z, y)
    direct = []
    for k in range(1, N):
        for h in range(2):
            copy = remote(
                mine.at[h], out.at[h, ring[h], across[h]],
                send1.at[h, k - 1], recv1.at[h, k - 1], line_device(1 - h, k),
            )
            copy.start()
            direct.append(copy)
    for h in range(2):
        out[h, ring[h], across[h]] = mine[h]
    yield
    for copy in direct:
        copy.wait_recv()
    sends += direct
    arriving = {}
    for step in range(1, N // 2 + 2):
        for h, d, p in CHAINS:
            sign = 1 - 2 * d
            if (h, d, p, step - 1) in arriving:
                arriving[h, d, p, step - 1].wait_recv()
            if step <= chain_length(d, p):
                ref = out.at[h, wrap(ring[h] - sign * (step - 1)), pl.ds(p * WIDTH, WIDTH)]
                copy = remote(
                    ref, ref, send2.at[h, d, step - 1, p], recv2.at[h, d, step - 1, p],
                    line_device(h, sign),
                )
                copy.start()
                sends.append(copy)
                arriving[h, d, p, step] = copy
        for h, d, p in CHAINS:
            if step <= chain_length(d, p) + 1 and (step > 1 or d == 0):
                visit(h, wrap(ring[h] - (1 - 2 * d) * (step - 1)), p)
        if step <= N // 2:
            yield


def gather_sems(*lead):
    shapes = [(2, N - 1)] * 2 + [CHAIN_SEMS] * 2
    return [pltpu.SemaphoreType.DMA(lead + shape) for shape in shapes]


def exchange(sources, targets, sends, send_sem, recv_sem, devices):
    copies = []
    for i, device in enumerate(devices):
        copy = remote(sources(i), targets(i), send_sem.at[i], recv_sem.at[i], device)
        copy.start()
        copies.append(copy)
    sends += copies
    return copies


def front_kernel(
    factor_ref, wide_ref, left_ref, gram_ref,
    got, partial_ref, landed, local, first, second, mine, slice_ref, *sems,
):
    y, z, tp = place()
    gather_sem, (s1, r1, s2, r2), gram_sem, spread_sem = (
        sems[:4], sems[4:8], sems[8:14], sems[14:],
    )
    greet(all_peers())
    sends = []

    partial_ref[...] = jnp.zeros_like(partial_ref)

    def add_terms(h, index, part):
        part = pl.ds(part * WIDTH, WIDTH)
        block = wide_ref[h, index, part].reshape(WIDTH * HALF, wide_ref.shape[-1])
        rows = got[h, index, part].reshape(WIDTH * HALF, RANK)
        partial_ref[...] += lax.dot_general(
            block, rows, (((0,), (0,)), ((), ())), preferred_element_type=jnp.float32
        )

    for _ in gather_plane(factor_ref, got, gather_sem, add_terms, sends):
        pass

    def rows(index):
        return pl.ds(pl.multiple_of(index * HALF, HALF), HALF)

    others = [tp_device(k) for k in range(1, N)]
    copies = exchange(
        lambda i: partial_ref.at[rows(wrap(tp + i + 1))], lambda i: landed.at[i], sends, s1, r1, others
    )
    total = partial_ref[rows(tp), :]
    for i, copy in enumerate(copies):
        copy.wait_recv()
        total = total + landed[i]
    left_ref[rows(tp), :] = total
    copies = exchange(
        lambda i: left_ref.at[rows(tp)], lambda i: left_ref.at[rows(tp)], sends, s2, r2, others
    )
    for copy in copies:
        copy.wait_recv()

    size = RANK // N
    at = pl.ds(pl.multiple_of(tp // 2 * BLOCK, BLOCK), BLOCK)
    left = left_ref[...]
    local[...] = full_dot(left_ref[:, at], left, ((0,), (0,)))
    half = RANK // 2
    start = lax.rem(tp, 2) * size
    ring, across = (y, z), (z, y)

    def piece(index, base=0):
        return pl.ds(pl.multiple_of(base + index * N, N), N)

    def lanes(h):
        return pl.ds(h * half, half)

    groups = [[line_device(1 - h, k) for k in range(1, N)] for h in range(2)]
    turned = [[line_device(h, k) for k in range(1, N)] for h in range(2)]
    copies = [
        exchange(
            lambda i, h=h: local.at[piece(wrap(across[h] + i + 1), start), lanes(h)],
            lambda i, h=h: first.at[h, i], sends, gram_sem[0].at[h], gram_sem[1].at[h], groups[h],
        )
        for h in range(2)
    ]
    for h in range(2):
        total = local[piece(across[h], start), h * half : (h + 1) * half]
        for i, copy in enumerate(copies[h]):
            copy.wait_recv()
            total = total + first[h, i]
        mine[h] = total
        second[h, ring[h]] = total
        copies[h] = exchange(
            lambda i, h=h: mine.at[h], lambda i, h=h: second.at[h, ring[h]],
            sends, gram_sem[2].at[h], gram_sem[3].at[h], turned[h],
        )
    for h in range(2):
        for copy in copies[h]:
            copy.wait_recv()
        total = second[h, 0]
        for k in range(1, N):
            total = total + second[h, k]
        slice_ref[piece(across[h]), h * half : (h + 1) * half] = total
        ref = slice_ref.at[piece(across[h]), lanes(h)]
        copies[h] = exchange(
            lambda i: ref, lambda i: ref, sends, gram_sem[4].at[h], gram_sem[5].at[h], groups[h]
        )
    for h in range(2):
        for copy in copies[h]:
            copy.wait_recv()

    sibling = (lax.axis_index("fsdp"), tp + 1 - 2 * lax.rem(tp, 2))

    def slab(index):
        return gram_ref.at[pl.ds(pl.multiple_of(index * size, size), size)]

    far = exchange(
        lambda i: slice_ref, lambda i: slab(tp), sends, spread_sem[0], spread_sem[1],
        [tp_device(2 * k) for k in range(1, N // 2)],
    )
    near = [remote(slice_ref, slab(tp), spread_sem[2].at[0], spread_sem[3].at[0], sibling)]
    near[0].start()
    gram_ref[pl.ds(pl.multiple_of(tp * size, size), size), :] = slice_ref[...]
    for k in (1, 3, 2):
        far[k - 1].wait_recv()
        ref = slab(wrap(tp - 2 * k))
        copy = remote(ref, ref, spread_sem[2].at[k], spread_sem[3].at[k], sibling)
        copy.start()
        near.append(copy)
    for copy in near:
        copy.wait_recv()
    for copy in sends + near:
        copy.wait_send()


def front(factor, wide):
    rows = wide.shape[-1]
    f32 = jnp.float32
    return pl.pallas_call(
        front_kernel,
        out_shape=(
            jax.ShapeDtypeStruct((rows, RANK), f32),
            jax.ShapeDtypeStruct((RANK, RANK), f32),
        ),
        in_specs=[VMEM, VMEM],
        out_specs=(VMEM, VMEM),
        scratch_shapes=[
            pltpu.VMEM((2, N, N, HALF, RANK), jnp.bfloat16),
            pltpu.VMEM((rows, RANK), f32),
            pltpu.VMEM((N - 1, HALF, RANK), f32),
            pltpu.VMEM((BLOCK, RANK), f32),
            pltpu.VMEM((2, N - 1, N, RANK // 2), f32),
            pltpu.VMEM((2, N, N, RANK // 2), f32),
            pltpu.VMEM((2, N, RANK // 2), f32),
            pltpu.VMEM((RANK // N, RANK), f32),
        ]
        + gather_sems()
        + [pltpu.SemaphoreType.DMA((N - 1,)) for _ in range(4)]
        + [pltpu.SemaphoreType.DMA((2, N - 1)) for _ in range(6)]
        + [pltpu.SemaphoreType.DMA((N // 2,)) for _ in range(4)],
        compiler_params=params(0),
        name="front",
    )(factor, wide)


BLOCK = 128
BASE = 8
PAUSES = (4, 10)
BLOCKS = RANK // BLOCK


def small_inverse(panel, first):
    wide = (BASE, BLOCK)
    entry = {
        (i, j): jnp.broadcast_to(panel[i : i + 1, first + j : first + j + 1], wide)
        for i in range(BASE)
        for j in range(i + 1)
    }
    lower, inverse, scale = {}, {}, {}
    for j in range(BASE):
        pivot = entry[j, j]
        guess = lax.rsqrt(pivot)
        scale[j] = guess * (1.5 - 0.5 * ((pivot * guess) * guess))
        for i in range(j + 1, BASE):
            lower[i, j] = entry[i, j] * scale[j]
        for i in range(j + 1, BASE):
            for m in range(j + 1, i + 1):
                entry[i, m] = entry[i, m] - lower[i, j] * lower[m, j]
    for j in range(BASE):
        inverse[j, j] = scale[j]
        for i in range(j + 1, BASE):
            total = lower[i, j] * inverse[j, j]
            for m in range(j + 1, i):
                total = total + lower[i, m] * inverse[m, j]
            inverse[i, j] = -(scale[i] * total)
    index = lax.broadcasted_iota(jnp.int32, wide, 0)
    columns, rows = [], []
    for j in range(BASE):
        column = jnp.zeros(wide, jnp.float32)
        row = jnp.zeros(wide, jnp.float32)
        for i in range(j, BASE):
            column = jnp.where(index == i, inverse[i, j], column)
        for i in range(j + 1):
            row = jnp.where(index == i, inverse[j, i], row)
        columns.append(column)
        rows.append(row)
    return columns, rows


def add_up(terms):
    while len(terms) > 1:
        terms = [sum(terms[i + 1 : i + 2], terms[i]) for i in range(0, len(terms), 2)]
    return terms[0]


def combine(factors, panel):
    return [
        add_up([factors[m] * piece[m : m + 1, :] for m in range(BASE)]) for piece in panel
    ]


def block_inverse(block):
    row = lax.broadcasted_iota(jnp.int32, (BLOCK, BLOCK), 0)
    column = lax.broadcasted_iota(jnp.int32, (BLOCK, BLOCK), 1)
    unit = jnp.where(row == column, 1.0, 0.0).astype(jnp.float32)
    count = BLOCK // BASE
    panels = [
        [matrix[b * BASE : (b + 1) * BASE, :] for matrix in (block, unit)] for b in range(count)
    ]
    solved = []
    for b in range(count):
        first = b * BASE
        columns, rows = small_inverse(panels[b][0], first)
        done = combine(columns, panels[b])
        solved.append(done[1])
        if b + 1 == count:
            break
        again = combine(rows, done)
        ahead = panels[b + 1]
        factors = [
            jnp.broadcast_to(ahead[0][:, first + m : first + m + 1], (BASE, BLOCK))
            for m in range(BASE)
        ]
        panels[b + 1] = [old - new for old, new in zip(ahead, combine(factors, again))]
        if b in PAUSES:
            yield
        if b + 2 == count:
            continue
        multiplier = jnp.concatenate([panels[c][0] for c in range(b + 2, count)], axis=0)
        parts = [jnp.concatenate(again, axis=1)]
        parts.append(jnp.zeros((BLOCK - first - BASE, 2 * BLOCK), jnp.float32))
        if first:
            parts.insert(0, jnp.zeros((first, 2 * BLOCK), jnp.float32))
        change = jnp.dot(
            multiplier, jnp.concatenate(parts, axis=0), precision=HIGHEST,
            preferred_element_type=jnp.float32,
        )
        for c in range(b + 2, count):
            at = (c - b - 2) * BASE
            panels[c] = [
                old - change[at : at + BASE, i * BLOCK : (i + 1) * BLOCK]
                for i, old in enumerate(panels[c])
            ]
    return jnp.where(row >= column, jnp.concatenate(solved, axis=0), 0.0)


def full_dot(x, y, dims):
    return lax.dot_general(
        x, y, (dims, ((), ())), precision=HIGHEST, preferred_element_type=jnp.float32
    )


def right_block(c, wide_ref, ortho_ref, mine_ref, right_ref, squares_ref, refs, sems, sends):
    chain, summed, landed = (ref.at[c] for ref in refs)
    send1, recv1, send2, recv2 = (sem.at[c] for sem in sems[:4])
    y, z, _ = place()
    ring, across = (y, z), (z, y)
    columns = slice(c * BLOCK, (c + 1) * BLOCK)

    def own(h, target, part):
        block = wide_ref[h, wrap(target), pl.ds(part * WIDTH, WIDTH)]
        product = jnp.dot(
            block.reshape(WIDTH * HALF, block.shape[-1]), ortho_ref[:, columns],
            preferred_element_type=jnp.float32,
        )
        return product.reshape(WIDTH, HALF, BLOCK)

    arriving = {}

    def pass_on(h, d, p, step):
        copy = remote(
            chain.at[h, d, step - 1, p], chain.at[h, d, step, p],
            send1.at[h, d, step - 1, p], recv1.at[h, d, step - 1, p], line_device(h, 1 - 2 * d),
        )
        copy.start()
        sends.append(copy)
        arriving[h, d, p, step] = copy

    for h, d, p in CHAINS:
        term = own(h, ring[h] + (1 - 2 * d) * chain_length(d, p), p)
        chain[h, d, 0, p] = term.astype(jnp.bfloat16)
        pass_on(h, d, p, 1)
    yield
    for step in range(1, N // 2):
        for h, d, p in CHAINS:
            length = chain_length(d, p)
            if step < length:
                term = own(h, ring[h] + (1 - 2 * d) * (length - step), p)
                arriving[h, d, p, step].wait_recv()
                term = term + chain[h, d, step, p].astype(jnp.float32)
                chain[h, d, step, p] = term.astype(jnp.bfloat16)
                pass_on(h, d, p, step + 1)
        yield
    for h in range(2):
        for p in range(PARTS):
            term = own(h, ring[h], p)
            for d in range(2):
                length = chain_length(d, p)
                arriving[h, d, p, length].wait_recv()
                term = term + chain[h, d, length, p].astype(jnp.float32)
            summed[h, p * WIDTH : (p + 1) * WIDTH] = term.astype(jnp.bfloat16)
    second = [
        exchange(
            lambda i, h=h: summed.at[h, wrap(across[h] + i + 1)], lambda i, h=h: landed.at[h, i],
            sends, send2.at[h], recv2.at[h], [line_device(1 - h, k) for k in range(1, N)],
        )
        for h in range(2)
    ]
    yield
    for h in range(2):
        total = summed[h, across[h]].astype(jnp.float32)
        for i, copy in enumerate(second[h]):
            copy.wait_recv()
            total = total + landed[h, i].astype(jnp.float32)
        mine_ref[c, h] = total.astype(jnp.bfloat16)

    def add_squares(h, index, part):
        block = right_ref[c, h, index, pl.ds(part * WIDTH, WIDTH)].astype(jnp.float32)
        block = block.reshape(WIDTH * HALF // N, N, BLOCK)
        squares_ref[:, columns] += jnp.sum(block * block, axis=0)

    yield from gather_plane(
        mine_ref.at[c], right_ref.at[c], [sem.at[c] for sem in sems[4:]], add_squares, sends
    )


def right_kernel(
    gram_ref, left_ref, wide_ref, ortho_ref, mine_ref, right_ref, squares_ref,
    rest, tail, chain, summed, landed, squares, spread, send, recv, *sems,
):
    greet(all_peers())
    sends, active = [], []

    def advance():
        for work in list(active):
            if next(work, active) is active:
                active.remove(work)

    rest[...] = gram_ref[...]
    tail[...] = left_ref[...]
    squares[...] = jnp.zeros_like(squares)
    for c in range(BLOCKS):
        at, end = c * BLOCK, (c + 1) * BLOCK
        elimination = block_inverse(rest[at:end, at:end])
        while True:
            try:
                next(elimination)
            except StopIteration as result:
                inverse = result.value
                break
            advance()
        done = full_dot(tail[:, at:end], inverse, ((1,), (1,)))
        ortho_ref[:, at:end] = done.astype(ortho_ref.dtype)
        advance()
        work = right_block(
            c, wide_ref, ortho_ref, mine_ref, right_ref, squares, (chain, summed, landed), sems, sends
        )
        next(work)
        active.append(work)
        if end == RANK:
            break
        panel = full_dot(inverse, rest[at:end, end:], ((1,), (0,)))
        for start in range(end, RANK, BLOCK):
            piece = panel[:, start - end : start - end + BLOCK]
            rest[start : start + BLOCK, start:] -= full_dot(
                piece, panel[:, start - end :], ((0,), (0,))
            )
        tail[:, end:] -= full_dot(done, panel, ((1,), (0,)))
    while active:
        advance()

    tp = lax.axis_index("tp")
    copies = exchange(
        lambda i: squares, lambda i: spread.at[tp], sends, send, recv,
        [tp_device(k) for k in range(1, N)],
    )
    spread[tp] = squares[...]
    for copy in copies:
        copy.wait_recv()
    total = spread[0]
    for k in range(1, N):
        total = total + spread[k]
    squares_ref[...] = total
    for copy in sends:
        copy.wait_send()


def make_right(gram, left, wide):
    rows = left.shape[0]
    f32, bf16 = jnp.float32, jnp.bfloat16
    return pl.pallas_call(
        right_kernel,
        out_shape=(
            jax.ShapeDtypeStruct((rows, RANK), bf16),
            jax.ShapeDtypeStruct((BLOCKS, 2, HALF, BLOCK), bf16),
            jax.ShapeDtypeStruct((BLOCKS, 2, N, N, HALF, BLOCK), bf16),
            jax.ShapeDtypeStruct((N, RANK), f32),
        ),
        in_specs=[VMEM] * 3,
        out_specs=(VMEM,) * 4,
        scratch_shapes=[
            pltpu.VMEM((RANK, RANK), f32),
            pltpu.VMEM((rows, RANK), f32),
            pltpu.VMEM((BLOCKS, 2, 2, N // 2 + 1, PARTS, WIDTH, HALF, BLOCK), bf16),
            pltpu.VMEM((BLOCKS, 2, N, HALF, BLOCK), bf16),
            pltpu.VMEM((BLOCKS, 2, N - 1, HALF, BLOCK), bf16),
            pltpu.VMEM((N, RANK), f32),
            pltpu.VMEM((N, N, RANK), f32),
            pltpu.SemaphoreType.DMA((N - 1,)),
            pltpu.SemaphoreType.DMA((N - 1,)),
            pltpu.SemaphoreType.DMA((BLOCKS,) + CHAIN_SEMS),
            pltpu.SemaphoreType.DMA((BLOCKS,) + CHAIN_SEMS),
            pltpu.SemaphoreType.DMA((BLOCKS, 2, N - 1)),
            pltpu.SemaphoreType.DMA((BLOCKS, 2, N - 1)),
        ]
        + gather_sems(BLOCKS),
        compiler_params=params(1),
        name="make_right",
    )(gram, left, wide)


def finish_kernel(
    squares_ref, first_ref, second_ref, mine_ref, ortho_ref, gradient_ref, momentum_ref,
    update_ref, new_ref, factor_ref, factor,
):
    squares = jnp.sum(squares_ref[...], axis=0, keepdims=True)
    norms = jnp.sqrt(squares + 1e-06)
    gain = math.sqrt(FFW) / norms
    ortho = ortho_ref[...]
    scaled = (ortho.astype(jnp.float32) * (norms / math.sqrt(FFW))).astype(jnp.bfloat16)
    stacked = jnp.concatenate([ortho, scaled], axis=0)
    group = 4
    for c in range(BLOCKS):
        columns = slice(c * BLOCK, (c + 1) * BLOCK)

        def joined(top, bottom):
            top = top.astype(jnp.float32) * gain[:, columns]
            bottom = bottom.astype(jnp.float32) * gain[:, columns]
            return [top, bottom[: ROWS - HALF]]

        factor_ref[:, columns] = jnp.concatenate(
            joined(mine_ref[c, 0], mine_ref[c, 1]), axis=0
        ).astype(jnp.bfloat16)
        for y in range(first_ref.shape[2]):
            for z in range(0, N, group):
                pieces = []
                for i in range(z, z + group):
                    pieces += joined(first_ref[c, 0, y, i], second_ref[c, 0, i, y])
                start = (y * N + z) * ROWS
                factor[start : start + group * ROWS, columns] = jnp.concatenate(
                    pieces, axis=0
                ).astype(jnp.bfloat16)
    combined = lax.dot_general(
        stacked, factor[...], (((1,), (1,)), ((), ())), preferred_element_type=jnp.float32
    )
    rows = ortho.shape[0]
    update_ref[...] = (math.sqrt(D / RANK) * combined[:rows]).astype(jnp.bfloat16)
    whole = momentum_ref[...] + gradient_ref[...].astype(jnp.float32)
    new_ref[...] = whole - 0.05 * combined[rows:]


def finish(squares, right, mine, ortho, gradient, momentum):
    steps = 2
    rows, columns = gradient.shape
    some = N // steps
    whole = lambda *shape: pl.BlockSpec(shape, lambda i: (0,) * len(shape))
    tile = pl.BlockSpec((rows, columns // steps), lambda i: (0, i))
    return pl.pallas_call(
        finish_kernel,
        grid=(steps,),
        out_shape=(
            jax.ShapeDtypeStruct((rows, columns), jnp.bfloat16),
            jax.ShapeDtypeStruct((rows, columns), jnp.float32),
            jax.ShapeDtypeStruct((ROWS, RANK), jnp.bfloat16),
        ),
        in_specs=[
            whole(N, RANK),
            pl.BlockSpec((BLOCKS, 1, some, N, HALF, BLOCK), lambda i: (0, 0, i, 0, 0, 0)),
            pl.BlockSpec((BLOCKS, 1, N, some, HALF, BLOCK), lambda i: (0, 1, 0, i, 0, 0)),
            whole(BLOCKS, 2, HALF, BLOCK),
            whole(rows, RANK),
            tile,
            tile,
        ],
        out_specs=(tile, tile, whole(ROWS, RANK)),
        scratch_shapes=[pltpu.VMEM((columns // steps, RANK), jnp.bfloat16)],
        compiler_params=pltpu.CompilerParams(vmem_limit_bytes=48 * 2**20),
        name="finish",
    )(squares, right, right, mine, ortho, gradient, momentum)


def body(gradient, momentum, right_factor):
    wide = (momentum + gradient.astype(jnp.float32)).astype(jnp.bfloat16)
    row_count = wide.shape[0]
    blocks = wide.T.reshape(N, N, ROWS, row_count)
    blocks = jnp.pad(blocks, ((0, 0), (0, 0), (0, PAD - ROWS), (0, 0)))
    blocks = jnp.stack([blocks[:, :, :HALF], jnp.swapaxes(blocks[:, :, HALF:], 0, 1)])
    factor = jnp.pad(right_factor, ((0, PAD - ROWS), (0, 0))).reshape(2, HALF, RANK)
    left, gram = front(factor, blocks)
    ortho, mine, right, squares = make_right(gram, left, blocks)
    return finish(squares, right, mine, ortho, gradient, momentum)


def solution(mesh):
    return jax.shard_map(
        body,
        mesh=mesh,
        in_specs=(P("fsdp", "tp"), P("fsdp", "tp"), P(("tp", "fsdp"), None)),
        out_specs=(P("fsdp", "tp"), P("fsdp", "tp"), P(("tp", "fsdp"), None)),
        check_vma=False,
    )
```

time: 782 us -> 182 us (0.23)
  waiting for transfers between devices: 397 us -> 0 us
  Pallas kernels: 0 us -> 176 us
  blocking collectives: 172 us -> 0 us
  other arithmetic: 122 us -> 1.42 us
  starting transfers between devices: 33.4 us -> 0 us
  local copies, waits for them, and re-layouts: 21.1 us -> 1.19 us
  matrix products: 18.5 us -> 0 us
  between operations: 17.4 us -> 0.71 us
    psum x2 -> x0, waiting for transfers between devices: 227 us -> none  [the longest x1 162 us: body(): lax.psum(jnp.dot(left.T, left, precision=lax.Precision.HIGHEST), 'fsdp')]
    pallas_call x0 -> x3, Pallas kernels: none -> 176 us  [the longest x1 103 us: make_right(): pl.pallas_call(right_kernel, out_shape=(jax.ShapeDtypeStruct((rows, RANK)...]
    all_gather x2 -> x0, waiting for transfers between devices: 169 us -> none  [the longest x1 91.4 us: body(): lax.all_gather(right_factor, 'fsdp', axis=0, tiled=True)]
    another operation x17 -> x1, other arithmetic: 119 us -> 0.05 us  [body(): jnp.stack([blocks[:, :, :HALF], jnp.swapaxes(blocks[:, :, HALF:], 0, 1)])]
    psum x1 -> x0, blocking collectives: 94.9 us -> none  [body(): norms = jnp.sqrt(lax.psum(squares, ('fsdp', 'tp')) + 1e-06)]
    unnamed x1 -> x0, blocking collectives: 76.8 us -> none
    unnamed x8 -> x0, starting transfers between devices: 33.2 us -> none
    another operation x13 -> x0, matrix products: 11.1 us -> none  [the longest x7 5.67 us: body(): jax.scipy.linalg.solve_triangular(lower, left.T, lower=True)]
  transfers between devices with their start and end apart: 12 -> 0, of which waited for: 4 -> 0; matrix products, arithmetic and copies ran while one was open for 0% -> 0% of each run, Pallas kernels for 0% -> 0%
where the time goes in v3:
time: 182 us; the launch traced here: 179 us
  Pallas kernels  176 us (97%)
    pallas_call x1, Pallas kernels, make_right(): pl.pallas_call(right_kernel, out_shape=(jax.ShapeDtypeStruct((rows, RANK)...  103 us
    pallas_call x1, Pallas kernels, front(): pl.pallas_call(front_kernel, out_shape=(jax.ShapeDtypeStruct((rows, RANK)...  70.3 us

profile of v3, /device:TPU:6, one launch (start us, length us, event | category | flops | bytes accessed | tf_op | source)
XLA Modules:
  0.0 179.1 jit_solution(7849579768067885429)
XLA Ops:
  0.6 0.8 pad.8
  1.4 1.4 fusion
  2.8 0.3 copy.7
  3.0 0.1 reshape.13
  3.1 0.1 fusion.1
  3.2 0.0 copy-start
  3.2 0.0 copy-start.1
  3.2 0.1 pad_maximum_fusion.wide_ref
  3.3 70.3 %front.1 = (f32[128,512]{1,0:T(8,128)S(1)}, f32[512,512]{1,0:T(8,128)S(1)}) custom-call(bf16[2,16,512]{2,1,0:T(8,128)(2,1)S(1)} %bitcast.9, bf16[2,8,8,16,128]{4,3,2,1,0:T(8,128)(2,1)S(1)} %pad_maximum_fusion.wide_ref), custom_call_target="tpu_custom_call" | custom-call | tf_op jit(solution)/shard_map/front/pallas_call | solution.py:252
  73.6 102.9 %make_right.1 = (bf16[128,512]{1,0:T(8,128)(2,1)S(1)}, bf16[4,2,16,128]{3,2,1,0:T(8,128)(2,1)S(1)}, bf16[4,2,8,8,16,128]{5,4,3,2,1,0:T(8,128)(2,1)S(1)}, f32[8,512]{1,0:T(8,128)S(1)}) custom-call(f32[512,512]{1,0:T(8,128)S(1)} %get-tuple-element.9.gram_ref, f32[128,512]{1,0:T(8,128)S(1)} %get-tuple-element.10.left_ref, ...), custom_call_target="tpu_custom_call" | custom-call | tf_op jit(solution)/shard_map/make_right/pallas_call | solution.py:524
  176.5 0.0 copy-done
  176.5 0.0 copy-done.1
  176.6 2.5 %finish.1 = (bf16[128,1792]{1,0:T(8,128)(2,1)}, f32[128,1792]{1,0:T(8,128)}, bf16[28,512]{1,0:T(8,128)(2,1)}) custom-call(f32[8,512]{1,0:T(8,128)S(1)} %get-tuple-element.11.squares_ref, bf16[4,2,8,8,16,128]{5,4,3,2,1,0:T(8,128)(2,1)S(1)} %get-tuple-element.12.first_ref.second_ref, ...), custom_call_target="tpu_custom_call" | custom-call | tf_op jit(solution)/shard_map/finish/pallas_call | solution.py:601
  (1 shorter events, 0.0 us)
Async XLA Ops:
  3.2 173.4 %copy-start = (f32[128,1792]{1,0:T(8,128)S(1)}, f32[128,1792]{1,0:T(8,128)}, u32[]{:S(2)}) copy-start(f32[128,1792]{1,0:T(8,128)} %momentum_ref.1) | copy-start | bytes 2752516
  3.2 173.4 %copy-start.1 = (bf16[128,1792]{1,0:T(8,128)(2,1)S(1)}, bf16[128,1792]{1,0:T(8,128)(2,1)}, u32[]{:S(2)}) copy-start(bf16[128,1792]{1,0:T(8,128)(2,1)} %gradient_ref.1) | copy-start | bytes 1376260

commit v4 on v3

v4 whole, which is shorter than its diff:
```python
import functools
import math

import jax
import jax.numpy as jnp
from jax import lax
from jax.experimental import pallas as pl
from jax.experimental.pallas import tpu as pltpu
from jax.sharding import PartitionSpec as P

D = 8192
FFW = 14336
RANK = 512
N = 8
ROWS = 28
PAD = 32
HALF = 16
MESH = pl.DeviceIdType.MESH
HIGHEST = lax.Precision.HIGHEST
VMEM = pl.BlockSpec(memory_space=pltpu.VMEM)


def params(collective_id):
    return pltpu.CompilerParams(
        collective_id=collective_id, has_side_effects=True, vmem_limit_bytes=48 * 2**20
    )


def wrap(index):
    return lax.rem(index + 2 * N, N)


def greet_start(peers):
    barrier = pltpu.get_barrier_semaphore()
    for peer in peers:
        pl.semaphore_signal(barrier, inc=1, device_id=peer, device_id_type=MESH)


def greet_end(peers):
    pl.semaphore_wait(pltpu.get_barrier_semaphore(), len(peers))


def remote(src, dst, send_sem, recv_sem, device):
    return pltpu.make_async_remote_copy(
        src_ref=src, dst_ref=dst, send_sem=send_sem, recv_sem=recv_sem,
        device_id=device, device_id_type=MESH,
    )


def place():
    fsdp = lax.axis_index("fsdp")
    return fsdp // N, lax.rem(fsdp, N), lax.axis_index("tp")


def line_device(axis, offset):
    y, z, tp = place()
    if axis == 0:
        return (wrap(y + offset) * N + z, tp)
    return (y * N + wrap(z + offset), tp)


def tp_device(offset):
    return (lax.axis_index("fsdp"), wrap(lax.axis_index("tp") + offset))


def all_peers():
    plane = [line_device(axis, k) for axis in range(2) for k in range(1, N)]
    return plane + [tp_device(k) for k in range(1, N)]


HALVES = (pl.ds(0, N // 2), pl.ds(N // 2, N // 2))
CHAINS = [(h, d) for h in range(2) for d in range(2)]


def signs(direction):
    return 1 - 2 * direction


def arrived(ref, sem, spare, device):
    remote(ref, ref, spare, sem, device).wait_recv()


def left_here(ref, sem, spare, device):
    remote(ref, ref, sem, spare, device).wait_send()


def exchange(source, target, send_sem, recv_sem, devices):
    for i, device in enumerate(devices):
        remote(source(i), target(i), send_sem, recv_sem, device).start()


def gather_plane(mine, out, sends, direct, landing, visit):
    y, z, _ = place()
    ring, across = (y, z), (z, y)
    for k in range(1, N):
        for h in range(2):
            remote(
                mine.at[h], out.at[h, ring[h], across[h]], sends.at[0], direct.at[h],
                line_device(1 - h, k),
            ).start()
    for h in range(2):
        out[h, ring[h], across[h]] = mine[h]
    for h in range(2):
        arrived(
            out.at[h, ring[h], pl.ds(0, N - 1)], direct.at[h], sends.at[0], line_device(1 - h, 1)
        )
    arriving = {}
    for step in range(1, N // 2 + 1):
        for h, d in CHAINS:
            if step > 1:
                arriving[h, d].wait_recv()
            index = wrap(ring[h] - signs(d) * (step - 1))
            ref = out.at[h, index] if step < N // 2 else out.at[h, index, HALVES[d]]
            arriving[h, d] = remote(
                ref, ref, sends.at[1], landing.at[h, d, step - 1], line_device(h, signs(d))
            )
            arriving[h, d].start()
        for h, d in CHAINS:
            if step > 1 or d == 0:
                visit(h, wrap(ring[h] - signs(d) * (step - 1)))
    for h, d in CHAINS:
        arriving[h, d].wait_recv()
        if d == 1:
            visit(h, wrap(ring[h] + N // 2))
    device = line_device(0, 1)
    left_here(out.at[:, 0, pl.ds(0, N - 1)], sends.at[0], direct.at[0], device)
    left_here(out.at[:, pl.ds(0, N - 1)], sends.at[1], direct.at[0], device)


def gather_sems():
    return [
        pltpu.SemaphoreType.DMA((2,)),
        pltpu.SemaphoreType.DMA((2,)),
        pltpu.SemaphoreType.DMA((2, 2, N // 2)),
    ]


def front_kernel(
    factor_ref, wide_ref, left_ref, gram_ref,
    got, partial_ref, landed, local, first, second, mine, slice_ref,
    gather_sends, direct, landing, sends, recvs,
):
    y, z, tp = place()
    greet_start(all_peers())
    partial_ref[...] = jnp.zeros_like(partial_ref)
    greet_end(all_peers())

    def add_terms(h, index):
        block = wide_ref[h, index].reshape(N * HALF, wide_ref.shape[-1])
        rows = got[h, index].reshape(N * HALF, RANK)
        partial_ref[...] += lax.dot_general(
            block, rows, (((0,), (0,)), ((), ())), preferred_element_type=jnp.float32
        )

    gather_plane(factor_ref, got, gather_sends, direct, landing, add_terms)

    def rows(index):
        return pl.ds(pl.multiple_of(index * HALF, HALF), HALF)

    others = [tp_device(k) for k in range(1, N)]
    exchange(
        lambda i: partial_ref.at[rows(wrap(tp + i + 1))], lambda i: landed.at[i],
        sends.at[0], recvs.at[0], others,
    )
    arrived(landed, recvs.at[0], sends.at[0], others[0])
    total = partial_ref[rows(tp), :]
    for i in range(N - 1):
        total = total + landed[i]
    left_ref[rows(tp), :] = total
    exchange(
        lambda i: left_ref.at[rows(tp)], lambda i: left_ref.at[rows(tp)],
        sends.at[1], recvs.at[1], others,
    )
    most = left_ref.at[pl.ds(0, (N - 1) * HALF)]
    arrived(most, recvs.at[1], sends.at[1], others[0])

    size = RANK // N
    at = pl.ds(pl.multiple_of(tp // 2 * BLOCK, BLOCK), BLOCK)
    local[...] = full_dot(left_ref[:, at], left_ref[...], ((0,), (0,)))
    start = lax.rem(tp, 2) * size

    def piece(index, base=0):
        return pl.ds(pl.multiple_of(base + index * N, N), N)

    along = [[line_device(axis, k) for k in range(1, N)] for axis in range(2)]
    exchange(
        lambda i: local.at[piece(wrap(z + i + 1), start)], lambda i: first.at[i],
        sends.at[2], recvs.at[2], along[1],
    )
    arrived(first, recvs.at[2], sends.at[2], along[1][0])
    total = local[piece(z, start), :]
    for i in range(N - 1):
        total = total + first[i]
    mine[...] = total
    second[y] = total
    exchange(
        lambda i: mine, lambda i: second.at[y], sends.at[3], recvs.at[3], along[0]
    )
    arrived(second.at[pl.ds(0, N - 1)], recvs.at[3], sends.at[3], along[0][0])
    total = second[0]
    for k in range(1, N):
        total = total + second[k]
    slice_ref[piece(z), :] = total
    ref = slice_ref.at[piece(z)]
    exchange(lambda i: ref, lambda i: ref, sends.at[4], recvs.at[4], along[1])
    some = slice_ref.at[pl.ds(0, (N - 1) * N)]
    arrived(some, recvs.at[4], sends.at[4], along[1][0])

    sibling = (lax.axis_index("fsdp"), tp + 1 - 2 * lax.rem(tp, 2))

    def slab(index, begin=0, count=size):
        begin = pl.multiple_of(wrap(index) * size + begin, size // 2)
        return gram_ref.at[pl.ds(begin, count)]

    far = []
    for d in range(2):
        far.append(
            remote(slice_ref, slab(tp), sends.at[5], recvs.at[5 + d], tp_device(2 * signs(d)))
        )
        far[d].start()
    remote(slice_ref, slab(tp), sends.at[5], recvs.at[9], sibling).start()
    gram_ref[pl.ds(pl.multiple_of(tp * size, size), size), :] = slice_ref[...]
    half = []
    for d in range(2):
        far[d].wait_recv()
        ref = slab(tp - 2 * signs(d), d * (size // 2), size // 2)
        half.append(remote(ref, ref, sends.at[5], recvs.at[7 + d], tp_device(2 * signs(d))))
        half[d].start()
        ref = slab(tp - 2 * signs(d))
        remote(ref, ref, sends.at[5], recvs.at[9], sibling).start()
    for d in range(2):
        half[d].wait_recv()
    ref = slab(tp + N // 2)
    remote(ref, ref, sends.at[5], recvs.at[9], sibling).start()
    arrived(gram_ref.at[pl.ds(0, N // 2 * size)], recvs.at[9], sends.at[5], sibling)

    left_here(landed, sends.at[0], recvs.at[0], sibling)
    left_here(most, sends.at[1], recvs.at[0], sibling)
    left_here(first, sends.at[2], recvs.at[0], sibling)
    left_here(second.at[pl.ds(0, N - 1)], sends.at[3], recvs.at[0], sibling)
    left_here(some, sends.at[4], recvs.at[0], sibling)
    left_here(gram_ref.at[pl.ds(0, (N - 1) * size)], sends.at[5], recvs.at[0], sibling)


def front(factor, wide):
    rows = wide.shape[-1]
    f32 = jnp.float32
    return pl.pallas_call(
        front_kernel,
        out_shape=(
            jax.ShapeDtypeStruct((rows, RANK), f32),
            jax.ShapeDtypeStruct((RANK, RANK), f32),
        ),
        in_specs=[VMEM, VMEM],
        out_specs=(VMEM, VMEM),
        scratch_shapes=[
            pltpu.VMEM((2, N, N, HALF, RANK), jnp.bfloat16),
            pltpu.VMEM((rows, RANK), f32),
            pltpu.VMEM((N - 1, HALF, RANK), f32),
            pltpu.VMEM((BLOCK, RANK), f32),
            pltpu.VMEM((N - 1, N, RANK), f32),
            pltpu.VMEM((N, N, RANK), f32),
            pltpu.VMEM((N, RANK), f32),
            pltpu.VMEM((RANK // N, RANK), f32),
        ]
        + gather_sems()
        + [pltpu.SemaphoreType.DMA((6,)), pltpu.SemaphoreType.DMA((10,))],
        compiler_params=params(0),
        name="front",
    )(factor, wide)


BLOCK = 128
BASE = 8


def small_inverse(panel, first):
    wide = (BASE, BLOCK)
    entry = {
        (i, j): jnp.broadcast_to(panel[i : i + 1, first + j : first + j + 1], wide)
        for i in range(BASE)
        for j in range(i + 1)
    }
    lower, inverse, scale = {}, {}, {}
    for j in range(BASE):
        pivot = entry[j, j]
        guess = lax.rsqrt(pivot)
        scale[j] = guess * (1.5 - 0.5 * ((pivot * guess) * guess))
        for i in range(j + 1, BASE):
            lower[i, j] = entry[i, j] * scale[j]
        for i in range(j + 1, BASE):
            for m in range(j + 1, i + 1):
                entry[i, m] = entry[i, m] - lower[i, j] * lower[m, j]
    for j in range(BASE):
        inverse[j, j] = scale[j]
        for i in range(j + 1, BASE):
            total = lower[i, j] * inverse[j, j]
            for m in range(j + 1, i):
                total = total + lower[i, m] * inverse[m, j]
            inverse[i, j] = -(scale[i] * total)
    index = lax.broadcasted_iota(jnp.int32, wide, 0)
    columns, rows = [], []
    for j in range(BASE):
        column = jnp.zeros(wide, jnp.float32)
        row = jnp.zeros(wide, jnp.float32)
        for i in range(j, BASE):
            column = jnp.where(index == i, inverse[i, j], column)
        for i in range(j + 1):
            row = jnp.where(index == i, inverse[j, i], row)
        columns.append(column)
        rows.append(row)
    return columns, rows


def add_up(terms):
    while len(terms) > 1:
        terms = [sum(terms[i + 1 : i + 2], terms[i]) for i in range(0, len(terms), 2)]
    return terms[0]


def combine(factors, panel):
    return [
        add_up([factors[m] * piece[m : m + 1, :] for m in range(BASE)]) for piece in panel
    ]


def block_inverse(block):
    row = lax.broadcasted_iota(jnp.int32, (BLOCK, BLOCK), 0)
    column = lax.broadcasted_iota(jnp.int32, (BLOCK, BLOCK), 1)
    unit = jnp.where(row == column, 1.0, 0.0).astype(jnp.float32)
    count = BLOCK // BASE
    panels = [
        [matrix[b * BASE : (b + 1) * BASE, :] for matrix in (block, unit)] for b in range(count)
    ]
    solved = []
    for b in range(count):
        first = b * BASE
        columns, rows = small_inverse(panels[b][0], first)
        done = combine(columns, panels[b])
        solved.append(done[1])
        if b + 1 == count:
            break
        again = combine(rows, done)
        ahead = panels[b + 1]
        factors = [
            jnp.broadcast_to(ahead[0][:, first + m : first + m + 1], (BASE, BLOCK))
            for m in range(BASE)
        ]
        panels[b + 1] = [old - new for old, new in zip(ahead, combine(factors, again))]
        if b + 2 == count:
            continue
        multiplier = jnp.concatenate([panels[c][0] for c in range(b + 2, count)], axis=0)
        parts = [jnp.concatenate(again, axis=1)]
        parts.append(jnp.zeros((BLOCK - first - BASE, 2 * BLOCK), jnp.float32))
        if first:
            parts.insert(0, jnp.zeros((first, 2 * BLOCK), jnp.float32))
        change = jnp.dot(
            multiplier, jnp.concatenate(parts, axis=0), precision=HIGHEST,
            preferred_element_type=jnp.float32,
        )
        for c in range(b + 2, count):
            at = (c - b - 2) * BASE
            panels[c] = [
                old - change[at : at + BASE, i * BLOCK : (i + 1) * BLOCK]
                for i, old in enumerate(panels[c])
            ]
    return jnp.where(row >= column, jnp.concatenate(solved, axis=0), 0.0)


def full_dot(x, y, dims):
    return lax.dot_general(
        x, y, (dims, ((), ())), precision=HIGHEST, preferred_element_type=jnp.float32
    )


def ortho_kernel(gram_ref, left_ref, out_ref, rest, tail):
    rest[...] = gram_ref[...]
    tail[...] = left_ref[...]
    for at in range(0, RANK, BLOCK):
        end = at + BLOCK
        inverse = block_inverse(rest[at:end, at:end])
        done = full_dot(tail[:, at:end], inverse, ((1,), (1,)))
        out_ref[:, at:end] = done.astype(out_ref.dtype)
        if end == RANK:
            break
        panel = full_dot(inverse, rest[at:end, end:], ((1,), (0,)))
        for start in range(end, RANK, BLOCK):
            piece = panel[:, start - end : start - end + BLOCK]
            rest[start : start + BLOCK, start:] -= full_dot(
                piece, panel[:, start - end :], ((0,), (0,))
            )
        tail[:, end:] -= full_dot(done, panel, ((1,), (0,)))


def orthonormalize(gram, left):
    return pl.pallas_call(
        ortho_kernel,
        out_shape=jax.ShapeDtypeStruct(left.shape, jnp.bfloat16),
        in_specs=[VMEM, VMEM],
        out_specs=VMEM,
        scratch_shapes=[
            pltpu.VMEM((RANK, RANK), jnp.float32),
            pltpu.VMEM(left.shape, jnp.float32),
        ],
        compiler_params=pltpu.CompilerParams(vmem_limit_bytes=48 * 2**20),
        name="orthonormalize",
    )(gram, left)


LINKS = N // 2 + 1


def right_kernel(
    wide_ref, ortho_ref, mine_ref, right_ref, squares_ref,
    chain, terms, summed, landed, squares, spread,
    gather_sends, direct, landing, sends, chain_recv, recvs,
):
    y, z, tp = place()
    ring, across = (y, z), (z, y)
    greet_start(all_peers())

    def own(h, target):
        block = wide_ref[h, wrap(target)].reshape(N * HALF, wide_ref.shape[-1])
        product = jnp.dot(block, ortho_ref[...], preferred_element_type=jnp.float32)
        return product.reshape(N, HALF, RANK)

    arriving = {}

    def pass_on(h, d, step):
        at = LINKS * d + step
        source, target = chain.at[h, at - 1], chain.at[h, at]
        if step == 1:
            source, target = chain.at[h, at - 1, HALVES[d]], chain.at[h, at, HALVES[d]]
        arriving[h, d] = remote(
            source, target, sends.at[0], chain_recv.at[h, d, step - 1], line_device(h, signs(d))
        )
        arriving[h, d].start()

    middle = N // 2
    for h in range(2):
        term = own(h, ring[h] + middle).astype(jnp.bfloat16)
        chain[h, 0, :middle] = term[:middle]
        chain[h, LINKS, middle:] = term[middle:]
    squares[...] = jnp.zeros_like(squares)
    greet_end(all_peers())
    for h, d in CHAINS:
        pass_on(h, d, 1)
    for step in range(1, middle):
        for i, (h, d) in enumerate(CHAINS):
            terms[i] = own(h, ring[h] + signs(d) * (middle - step))
        for i, (h, d) in enumerate(CHAINS):
            at = LINKS * d + step
            arriving[h, d].wait_recv()
            if step == 1:
                here = slice(0, middle) if d == 0 else slice(middle, N)
                rest = slice(middle, N) if d == 0 else slice(0, middle)
                total = terms[i, here] + chain[h, at, here].astype(jnp.float32)
                chain[h, at, here] = total.astype(jnp.bfloat16)
                chain[h, at, rest] = terms[i, rest].astype(jnp.bfloat16)
            else:
                total = terms[i] + chain[h, at].astype(jnp.float32)
                chain[h, at] = total.astype(jnp.bfloat16)
            pass_on(h, d, step + 1)
    for h in range(2):
        terms[h] = own(h, ring[h])
    for h in range(2):
        for d in range(2):
            arriving[h, d].wait_recv()
        total = terms[h] + chain[h, middle].astype(jnp.float32)
        total = total + chain[h, LINKS + middle].astype(jnp.float32)
        summed[h] = total.astype(jnp.bfloat16)
        exchange(
            lambda i: summed.at[h, wrap(across[h] + i + 1)], lambda i: landed.at[h, i],
            sends.at[1], recvs.at[h], [line_device(1 - h, k) for k in range(1, N)],
        )
    device = line_device(0, 1)
    for h in range(2):
        arrived(landed.at[h], recvs.at[h], sends.at[1], device)
        total = summed[h, across[h]].astype(jnp.float32)
        for i in range(N - 1):
            total = total + landed[h, i].astype(jnp.float32)
        mine_ref[h] = total.astype(jnp.bfloat16)

    def add_squares(h, index):
        block = right_ref[h, index].astype(jnp.float32).reshape(N * HALF // N, N, RANK)
        squares[...] += jnp.sum(block * block, axis=0)

    gather_plane(mine_ref, right_ref, gather_sends, direct, landing, add_squares)

    exchange(
        lambda i: squares, lambda i: spread.at[tp], sends.at[2], recvs.at[2],
        [tp_device(k) for k in range(1, N)],
    )
    spread[tp] = squares[...]
    others = spread.at[pl.ds(0, N - 1)]
    arrived(others, recvs.at[2], sends.at[2], device)
    total = spread[0]
    for k in range(1, N):
        total = total + spread[k]
    squares_ref[...] = total
    left_here(chain.at[:, pl.ds(0, N - 1)], sends.at[0], recvs.at[0], device)
    left_here(landed, sends.at[1], recvs.at[0], device)
    left_here(others, sends.at[2], recvs.at[0], device)


def make_right(wide, ortho):
    f32, bf16 = jnp.float32, jnp.bfloat16
    return pl.pallas_call(
        right_kernel,
        out_shape=(
            jax.ShapeDtypeStruct((2, HALF, RANK), bf16),
            jax.ShapeDtypeStruct((2, N, N, HALF, RANK), bf16),
            jax.ShapeDtypeStruct((N, RANK), f32),
        ),
        in_specs=[VMEM] * 2,
        out_specs=(VMEM,) * 3,
        scratch_shapes=[
            pltpu.VMEM((2, 2 * LINKS, N, HALF, RANK), bf16),
            pltpu.VMEM((4, N, HALF, RANK), f32),
            pltpu.VMEM((2, N, HALF, RANK), bf16),
            pltpu.VMEM((2, N - 1, HALF, RANK), bf16),
            pltpu.VMEM((N, RANK), f32),
            pltpu.VMEM((N, N, RANK), f32),
        ]
        + gather_sems()
        + [
            pltpu.SemaphoreType.DMA((3,)),
            pltpu.SemaphoreType.DMA((2, 2, N // 2)),
            pltpu.SemaphoreType.DMA((3,)),
        ],
        compiler_params=params(1),
        name="make_right",
    )(wide, ortho)


def finish_kernel(
    squares_ref, first_ref, second_ref, mine_ref, ortho_ref, gradient_ref, momentum_ref,
    update_ref, new_ref, factor_ref, factor,
):
    squares = jnp.sum(squares_ref[...], axis=0, keepdims=True)
    norms = jnp.sqrt(squares + 1e-06)
    gain = math.sqrt(FFW) / norms
    ortho = ortho_ref[...]
    scaled = (ortho.astype(jnp.float32) * (norms / math.sqrt(FFW))).astype(jnp.bfloat16)
    stacked = jnp.concatenate([ortho, scaled], axis=0)
    group = 4

    def joined(top, bottom):
        top = top.astype(jnp.float32) * gain
        bottom = bottom.astype(jnp.float32) * gain
        return [top, bottom[: ROWS - HALF]]

    factor_ref[...] = jnp.concatenate(joined(mine_ref[0], mine_ref[1]), axis=0).astype(jnp.bfloat16)
    for y in range(first_ref.shape[1]):
        for z in range(0, N, group):
            pieces = []
            for i in range(z, z + group):
                pieces += joined(first_ref[0, y, i], second_ref[0, i, y])
            start = (y * N + z) * ROWS
            factor[start : start + group * ROWS, :] = jnp.concatenate(
                pieces, axis=0
            ).astype(jnp.bfloat16)
    combined = lax.dot_general(
        stacked, factor[...], (((1,), (1,)), ((), ())), preferred_element_type=jnp.float32
    )
    rows = ortho.shape[0]
    update_ref[...] = (math.sqrt(D / RANK) * combined[:rows]).astype(jnp.bfloat16)
    whole = momentum_ref[...] + gradient_ref[...].astype(jnp.float32)
    new_ref[...] = whole - 0.05 * combined[rows:]


def finish(squares, right, mine, ortho, gradient, momentum):
    steps = 2
    rows, columns = gradient.shape
    some = N // steps
    whole = lambda *shape: pl.BlockSpec(shape, lambda i: (0,) * len(shape))
    tile = pl.BlockSpec((rows, columns // steps), lambda i: (0, i))
    return pl.pallas_call(
        finish_kernel,
        grid=(steps,),
        out_shape=(
            jax.ShapeDtypeStruct((rows, columns), jnp.bfloat16),
            jax.ShapeDtypeStruct((rows, columns), jnp.float32),
            jax.ShapeDtypeStruct((ROWS, RANK), jnp.bfloat16),
        ),
        in_specs=[
            whole(N, RANK),
            pl.BlockSpec((1, some, N, HALF, RANK), lambda i: (0, i, 0, 0, 0)),
            pl.BlockSpec((1, N, some, HALF, RANK), lambda i: (1, 0, i, 0, 0)),
            whole(2, HALF, RANK),
            whole(rows, RANK),
            tile,
            tile,
        ],
        out_specs=(tile, tile, whole(ROWS, RANK)),
        scratch_shapes=[pltpu.VMEM((columns // steps, RANK), jnp.bfloat16)],
        compiler_params=pltpu.CompilerParams(vmem_limit_bytes=48 * 2**20),
        name="finish",
    )(squares, right, right, mine, ortho, gradient, momentum)


def body(gradient, momentum, right_factor):
    wide = (momentum + gradient.astype(jnp.float32)).astype(jnp.bfloat16)
    row_count = wide.shape[0]
    blocks = wide.T.reshape(N, N, ROWS, row_count)
    blocks = jnp.pad(blocks, ((0, 0), (0, 0), (0, PAD - ROWS), (0, 0)))
    blocks = jnp.stack([blocks[:, :, :HALF], jnp.swapaxes(blocks[:, :, HALF:], 0, 1)])
    factor = jnp.pad(right_factor, ((0, PAD - ROWS), (0, 0))).reshape(2, HALF, RANK)
    left, gram = front(factor, blocks)
    ortho = orthonormalize(gram, left)
    mine, right, squares = make_right(blocks, ortho)
    return finish(squares, right, mine, ortho, gradient, momentum)


def solution(mesh):
    return jax.shard_map(
        body,
        mesh=mesh,
        in_specs=(P("fsdp", "tp"), P("fsdp", "tp"), P(("tp", "fsdp"), None)),
        out_specs=(P("fsdp", "tp"), P("fsdp", "tp"), P(("tp", "fsdp"), None)),
        check_vma=False,
    )
```

time: 182 us -> 162 us (0.89)
  Pallas kernels: 176 us -> 156 us
    pallas_call x1 -> x2, Pallas kernels: 103 us -> 79.2 us  [the longest x1 59.4 us: make_right(): pl.pallas_call(right_kernel, out_shape=(jax.ShapeDtypeStruct((2, HALF, RA...]
    pallas_call x1, Pallas kernels: 70.3 us -> 74.6 us  [front(): pl.pallas_call(front_kernel, out_shape=(jax.ShapeDtypeStruct((rows, RANK)...]
where the time goes in v4:
time: 162 us; the launch traced here: 159 us
  Pallas kernels  156 us (96%)
    pallas_call x1, Pallas kernels, front(): pl.pallas_call(front_kernel, out_shape=(jax.ShapeDtypeStruct((rows, RANK)...  74.6 us
    pallas_call x1, Pallas kernels, make_right(): pl.pallas_call(right_kernel, out_shape=(jax.ShapeDtypeStruct((2, HALF, RA...  59.4 us
    pallas_call x1, Pallas kernels, orthonormalize(): pl.pallas_call(ortho_kernel, out_shape=jax.ShapeDtypeStruct(left.shape, j...  19.8 us

profile of v4, /device:TPU:6, one launch (start us, length us, event | category | flops | bytes accessed | tf_op | source)
XLA Modules:
  0.0 159.4 jit_solution(17620355248678606326)
XLA Ops:
  0.6 0.8 pad.9
  1.4 1.4 fusion
  2.8 0.3 copy.7
  3.0 0.1 reshape.12
  3.1 0.1 fusion.1
  3.2 0.0 copy-start
  3.2 0.0 copy-start.1
  3.2 0.1 pad_maximum_fusion.wide_ref
  3.3 74.6 %front.1 = (f32[128,512]{1,0:T(8,128)S(1)}, f32[512,512]{1,0:T(8,128)S(1)}) custom-call(bf16[2,16,512]{2,1,0:T(8,128)(2,1)S(1)} %bitcast.9, bf16[2,8,8,16,128]{4,3,2,1,0:T(8,128)(2,1)S(1)} %pad_maximum_fusion.wide_ref), custom_call_target="tpu_custom_call" | custom-call | tf_op jit(solution)/shard_map/front/pallas_call | solution.py:248
  77.9 19.8 %orthonormalize.1.ortho_ref = bf16[128,512]{1,0:T(8,128)(2,1)S(1)} custom-call(f32[512,512]{1,0:T(8,128)S(1)} %get-tuple-element.8.gram_ref, f32[128,512]{1,0:T(8,128)S(1)} %get-tuple-element.9.left_ref), custom_call_target="tpu_custom_call" | custom-call | tf_op jit(solution)/shard_map/orthonormalize/pallas_call | solution.py:396
  97.7 59.4 %make_right.1 = (bf16[2,16,512]{2,1,0:T(8,128)(2,1)S(1)}, bf16[2,8,8,16,512]{4,3,2,1,0:T(8,128)(2,1)S(1)}, f32[8,512]{1,0:T(8,128)S(1)}) custom-call(bf16[2,8,8,16,128]{4,3,2,1,0:T(8,128)(2,1)S(1)} %pad_maximum_fusion.wide_ref, bf16[128,512]{1,0:T(8,128)(2,1)S(1)} %orthonormalize.1.ortho_ref), custom_call_target="tpu_custom_call" | custom-call | tf_op jit(solution)/shard_map/make_right/pallas_call | solution.py:508
  157.2 0.0 copy-done
  157.2 0.0 copy-done.1
  157.2 2.2 %finish.1 = (bf16[128,1792]{1,0:T(8,128)(2,1)}, f32[128,1792]{1,0:T(8,128)}, bf16[28,512]{1,0:T(8,128)(2,1)}) custom-call(f32[8,512]{1,0:T(8,128)S(1)} %get-tuple-element.10.squares_ref, bf16[2,8,8,16,512]{4,3,2,1,0:T(8,128)(2,1)S(1)} %get-tuple-element.11.first_ref.second_ref, bf16[2,8,8,16,512]{4,3,2,1,0:T(8,128)(2,1)S(1)} %get-tuple-element.11.first_ref.second_ref, ...), custom_call_target="tpu_custom_call" | custom-call | tf_op jit(solution)/shard_map/finish/pallas_call | solution.py:578
  (1 shorter events, 0.0 us)
Async XLA Ops:
  3.2 154.0 %copy-start = (f32[128,1792]{1,0:T(8,128)S(1)}, f32[128,1792]{1,0:T(8,128)}, u32[]{:S(2)}) copy-start(f32[128,1792]{1,0:T(8,128)} %momentum_ref.1) | copy-start | bytes 2752516
  3.2 154.0 %copy-start.1 = (bf16[128,1792]{1,0:T(8,128)(2,1)S(1)}, bf16[128,1792]{1,0:T(8,128)(2,1)}, u32[]{:S(2)}) copy-start(bf16[128,1792]{1,0:T(8,128)(2,1)} %gradient_ref.1) | copy-start | bytes 1376260

commit v5 on v4

--- a/solution.py
+++ b/solution.py
@@ -69,7 +69,11 @@
 
 
 HALVES = (pl.ds(0, N // 2), pl.ds(N // 2, N // 2))
-CHAINS = [(h, d) for h in range(2) for d in range(2)]
+CHAINS = [(h, d, p) for q in range(2) for h in range(2) for d in range(2) for p in [d ^ q]]
+
+
+def chain_length(direction, part):
+    return N // 2 if direction == part else N // 2 - 1
 
 
 def signs(direction):
@@ -105,33 +109,34 @@
             out.at[h, ring[h], pl.ds(0, N - 1)], direct.at[h], sends.at[0], line_device(1 - h, 1)
         )
     arriving = {}
-    for step in range(1, N // 2 + 1):
-        for h, d in CHAINS:
-            if step > 1:
-                arriving[h, d].wait_recv()
-            index = wrap(ring[h] - signs(d) * (step - 1))
-            ref = out.at[h, index] if step < N // 2 else out.at[h, index, HALVES[d]]
-            arriving[h, d] = remote(
-                ref, ref, sends.at[1], landing.at[h, d, step - 1], line_device(h, signs(d))
-            )
-            arriving[h, d].start()
-        for h, d in CHAINS:
-            if step > 1 or d == 0:
-                visit(h, wrap(ring[h] - signs(d) * (step - 1)))
-    for h, d in CHAINS:
-        arriving[h, d].wait_recv()
-        if d == 1:
-            visit(h, wrap(ring[h] + N // 2))
     device = line_device(0, 1)
+    for step in range(1, N // 2 + 2):
+        for h, d, p in CHAINS:
+            if step == 1 and (h, d, p) == CHAINS[4]:
+                for i, q in [(0, 0), (0, 1), (1, 0), (1, 1)]:
+                    visit(i, ring[i], q)
+                left_here(out.at[:, 0], sends.at[2], direct.at[0], device)
+            if 1 < step <= chain_length(d, p) + 1:
+                arriving[h, d, p].wait_recv()
+            if step <= chain_length(d, p):
+                ref = out.at[h, wrap(ring[h] - signs(d) * (step - 1)), HALVES[p]]
+                arriving[h, d, p] = remote(
+                    ref, ref, sends.at[2 if step == 1 and d == p else 1],
+                    landing.at[h, d, p, step - 1], line_device(h, signs(d)),
+                )
+                arriving[h, d, p].start()
+        for h, d, p in CHAINS:
+            if 1 < step <= chain_length(d, p) + 1:
+                visit(h, wrap(ring[h] - signs(d) * (step - 1)), p)
     left_here(out.at[:, 0, pl.ds(0, N - 1)], sends.at[0], direct.at[0], device)
-    left_here(out.at[:, pl.ds(0, N - 1)], sends.at[1], direct.at[0], device)
+    left_here(out.at[:, pl.ds(0, N - 2)], sends.at[1], direct.at[0], device)
 
 
 def gather_sems():
     return [
+        pltpu.SemaphoreType.DMA((3,)),
         pltpu.SemaphoreType.DMA((2,)),
-        pltpu.SemaphoreType.DMA((2,)),
-        pltpu.SemaphoreType.DMA((2, 2, N // 2)),
+        pltpu.SemaphoreType.DMA((2, 2, 2, N // 2)),
     ]
 
 
@@ -145,9 +150,9 @@
     partial_ref[...] = jnp.zeros_like(partial_ref)
     greet_end(all_peers())
 
-    def add_terms(h, index):
-        block = wide_ref[h, index].reshape(N * HALF, wide_ref.shape[-1])
-        rows = got[h, index].reshape(N * HALF, RANK)
+    def add_terms(h, index, part):
+        block = wide_ref[h, index, HALVES[part]].reshape(N // 2 * HALF, wide_ref.shape[-1])
+        rows = got[h, index, HALVES[part]].reshape(N // 2 * HALF, RANK)
         partial_ref[...] += lax.dot_general(
             block, rows, (((0,), (0,)), ((), ())), preferred_element_type=jnp.float32
         )
@@ -178,33 +183,43 @@
     at = pl.ds(pl.multiple_of(tp // 2 * BLOCK, BLOCK), BLOCK)
     local[...] = full_dot(left_ref[:, at], left_ref[...], ((0,), (0,)))
     start = lax.rem(tp, 2) * size
+    width = RANK // 2
+    ring, across = (y, z), (z, y)
 
     def piece(index, base=0):
         return pl.ds(pl.multiple_of(base + index * N, N), N)
 
+    def lanes(h):
+        return pl.ds(h * width, width)
+
     along = [[line_device(axis, k) for k in range(1, N)] for axis in range(2)]
-    exchange(
-        lambda i: local.at[piece(wrap(z + i + 1), start)], lambda i: first.at[i],
-        sends.at[2], recvs.at[2], along[1],
-    )
-    arrived(first, recvs.at[2], sends.at[2], along[1][0])
-    total = local[piece(z, start), :]
-    for i in range(N - 1):
-        total = total + first[i]
-    mine[...] = total
-    second[y] = total
-    exchange(
-        lambda i: mine, lambda i: second.at[y], sends.at[3], recvs.at[3], along[0]
-    )
-    arrived(second.at[pl.ds(0, N - 1)], recvs.at[3], sends.at[3], along[0][0])
-    total = second[0]
-    for k in range(1, N):
-        total = total + second[k]
-    slice_ref[piece(z), :] = total
-    ref = slice_ref.at[piece(z)]
-    exchange(lambda i: ref, lambda i: ref, sends.at[4], recvs.at[4], along[1])
-    some = slice_ref.at[pl.ds(0, (N - 1) * N)]
-    arrived(some, recvs.at[4], sends.at[4], along[1][0])
+    for h in range(2):
+        exchange(
+            lambda i: local.at[piece(wrap(across[h] + i + 1), start), lanes(h)],
+            lambda i: first.at[h, i], sends.at[2], recvs.at[2 + h], along[1 - h],
+        )
+    for h in range(2):
+        arrived(first.at[h], recvs.at[2 + h], sends.at[2], others[0])
+        total = local[piece(across[h], start), h * width : (h + 1) * width]
+        for i in range(N - 1):
+            total = total + first[h, i]
+        mine[h] = total
+        second[h, ring[h]] = total
+        exchange(
+            lambda i: mine.at[h], lambda i: second.at[h, ring[h]],
+            sends.at[3], recvs.at[4 + h], along[h],
+        )
+    for h in range(2):
+        arrived(second.at[h, pl.ds(0, N - 1)], recvs.at[4 + h], sends.at[3], others[0])
+        total = second[h, 0]
+        for k in range(1, N):
+            total = total + second[h, k]
+        slice_ref[piece(across[h]), h * width : (h + 1) * width] = total
+        ref = slice_ref.at[piece(across[h]), lanes(h)]
+        exchange(lambda i: ref, lambda i: ref, sends.at[4], recvs.at[6 + h], along[1 - h])
+    some = pl.ds(0, (N - 1) * N)
+    for h in range(2):
+        arrived(slice_ref.at[some, lanes(h)], recvs.at[6 + h], sends.at[4], others[0])
 
     sibling = (lax.axis_index("fsdp"), tp + 1 - 2 * lax.rem(tp, 2))
 
@@ -215,30 +230,30 @@
     far = []
     for d in range(2):
         far.append(
-            remote(slice_ref, slab(tp), sends.at[5], recvs.at[5 + d], tp_device(2 * signs(d)))
+            remote(slice_ref, slab(tp), sends.at[5], recvs.at[8 + d], tp_device(2 * signs(d)))
         )
         far[d].start()
-    remote(slice_ref, slab(tp), sends.at[5], recvs.at[9], sibling).start()
+    remote(slice_ref, slab(tp), sends.at[5], recvs.at[12], sibling).start()
     gram_ref[pl.ds(pl.multiple_of(tp * size, size), size), :] = slice_ref[...]
     half = []
     for d in range(2):
         far[d].wait_recv()
         ref = slab(tp - 2 * signs(d), d * (size // 2), size // 2)
-        half.append(remote(ref, ref, sends.at[5], recvs.at[7 + d], tp_device(2 * signs(d))))
+        half.append(remote(ref, ref, sends.at[5], recvs.at[10 + d], tp_device(2 * signs(d))))
         half[d].start()
         ref = slab(tp - 2 * signs(d))
-        remote(ref, ref, sends.at[5], recvs.at[9], sibling).start()
+        remote(ref, ref, sends.at[5], recvs.at[12], sibling).start()
     for d in range(2):
         half[d].wait_recv()
     ref = slab(tp + N // 2)
-    remote(ref, ref, sends.at[5], recvs.at[9], sibling).start()
-    arrived(gram_ref.at[pl.ds(0, N // 2 * size)], recvs.at[9], sends.at[5], sibling)
+    remote(ref, ref, sends.at[5], recvs.at[12], sibling).start()
+    arrived(gram_ref.at[pl.ds(0, N // 2 * size)], recvs.at[12], sends.at[5], sibling)
 
     left_here(landed, sends.at[0], recvs.at[0], sibling)
     left_here(most, sends.at[1], recvs.at[0], sibling)
     left_here(first, sends.at[2], recvs.at[0], sibling)
-    left_here(second.at[pl.ds(0, N - 1)], sends.at[3], recvs.at[0], sibling)
-    left_here(some, sends.at[4], recvs.at[0], sibling)
+    left_here(second.at[:, pl.ds(0, N - 1)], sends.at[3], recvs.at[0], sibling)
+    left_here(slice_ref.at[some], sends.at[4], recvs.at[0], sibling)
     left_here(gram_ref.at[pl.ds(0, (N - 1) * size)], sends.at[5], recvs.at[0], sibling)
 
 
@@ -258,13 +273,13 @@
             pltpu.VMEM((rows, RANK), f32),
             pltpu.VMEM((N - 1, HALF, RANK), f32),
             pltpu.VMEM((BLOCK, RANK), f32),
-            pltpu.VMEM((N - 1, N, RANK), f32),
-            pltpu.VMEM((N, N, RANK), f32),
-            pltpu.VMEM((N, RANK), f32),
+            pltpu.VMEM((2, N - 1, N, RANK // 2), f32),
+            pltpu.VMEM((2, N, N, RANK // 2), f32),
+            pltpu.VMEM((2, N, RANK // 2), f32),
             pltpu.VMEM((RANK // N, RANK), f32),
         ]
         + gather_sems()
-        + [pltpu.SemaphoreType.DMA((6,)), pltpu.SemaphoreType.DMA((10,))],
+        + [pltpu.SemaphoreType.DMA((6,)), pltpu.SemaphoreType.DMA((13,))],
         compiler_params=params(0),
         name="front",
     )(factor, wide)
@@ -419,61 +434,69 @@
     ring, across = (y, z), (z, y)
     greet_start(all_peers())
 
-    def own(h, target):
-        block = wide_ref[h, wrap(target)].reshape(N * HALF, wide_ref.shape[-1])
-        product = jnp.dot(block, ortho_ref[...], preferred_element_type=jnp.float32)
-        return product.reshape(N, HALF, RANK)
+    def own(h, target, part):
+        block = wide_ref[h, wrap(target), HALVES[part]]
+        product = jnp.dot(
+            block.reshape(N // 2 * HALF, block.shape[-1]), ortho_ref[...],
+            preferred_element_type=jnp.float32,
+        )
+        return product.reshape(N // 2, HALF, RANK)
 
     arriving = {}
 
-    def pass_on(h, d, step):
-        at = LINKS * d + step
-        source, target = chain.at[h, at - 1], chain.at[h, at]
-        if step == 1:
-            source, target = chain.at[h, at - 1, HALVES[d]], chain.at[h, at, HALVES[d]]
-        arriving[h, d] = remote(
-            source, target, sends.at[0], chain_recv.at[h, d, step - 1], line_device(h, signs(d))
-        )
-        arriving[h, d].start()
-
-    middle = N // 2
-    for h in range(2):
-        term = own(h, ring[h] + middle).astype(jnp.bfloat16)
-        chain[h, 0, :middle] = term[:middle]
-        chain[h, LINKS, middle:] = term[middle:]
+    def slot(h, d, p, step):
+        return chain.at[h, LINKS * d + step, HALVES[p]]
+
+    def pass_on(h, d, p, step):
+        arriving[h, d, p] = remote(
+            slot(h, d, p, step - 1), slot(h, d, p, step),
+            sends.at[3 if step == 1 and d == p else 0], chain_recv.at[h, d, p, step - 1],
+            line_device(h, signs(d)),
+        )
+        arriving[h, d, p].start()
+
+    def prepare(step):
+        for h, d, p in CHAINS:
+            if step < chain_length(d, p):
+                target = ring[h] + signs(d) * (chain_length(d, p) - step)
+                terms[h, d, HALVES[p]] = own(h, target, p)
+
+    for h, d, p in CHAINS:
+        term = own(h, ring[h] + signs(d) * chain_length(d, p), p)
+        slot(h, d, p, 0)[...] = term.astype(jnp.bfloat16)
     squares[...] = jnp.zeros_like(squares)
     greet_end(all_peers())
-    for h, d in CHAINS:
-        pass_on(h, d, 1)
-    for step in range(1, middle):
-        for i, (h, d) in enumerate(CHAINS):
-            terms[i] = own(h, ring[h] + signs(d) * (middle - step))
-        for i, (h, d) in enumerate(CHAINS):
-            at = LINKS * d + step
-            arriving[h, d].wait_recv()
-            if step == 1:
-                here = slice(0, middle) if d == 0 else slice(middle, N)
-                rest = slice(middle, N) if d == 0 else slice(0, middle)
-                total = terms[i, here] + chain[h, at, here].astype(jnp.float32)
-                chain[h, at, here] = total.astype(jnp.bfloat16)
-                chain[h, at, rest] = terms[i, rest].astype(jnp.bfloat16)
-            else:
-                total = terms[i] + chain[h, at].astype(jnp.float32)
-                chain[h, at] = total.astype(jnp.bfloat16)
-            pass_on(h, d, step + 1)
-    for h in range(2):
-        terms[h] = own(h, ring[h])
-    for h in range(2):
-        for d in range(2):
-            arriving[h, d].wait_recv()
-        total = terms[h] + chain[h, middle].astype(jnp.float32)
-        total = total + chain[h, LINKS + middle].astype(jnp.float32)
-        summed[h] = total.astype(jnp.bfloat16)
+    device = line_device(0, 1)
+    for h, d, p in CHAINS[:4]:
+        pass_on(h, d, p, 1)
+    prepare(1)
+    left_here(chain.at[:, 0], sends.at[3], recvs.at[0], device)
+    for h, d, p in CHAINS[4:]:
+        pass_on(h, d, p, 1)
+    for step in range(1, N // 2):
+        for h, d, p in CHAINS:
+            if step < chain_length(d, p):
+                arriving[h, d, p].wait_recv()
+                ref = slot(h, d, p, step)
+                total = terms[h, d, HALVES[p]] + ref[...].astype(jnp.float32)
+                ref[...] = total.astype(jnp.bfloat16)
+                pass_on(h, d, p, step + 1)
+        prepare(step + 1)
+    for h, d, p in CHAINS[4:]:
+        arriving[h, d, p].wait_recv()
+        ref = slot(h, d, p, chain_length(d, p))
+        terms[h, 0, HALVES[p]] = own(h, ring[h], p) + ref[...].astype(jnp.float32)
+    for h in range(2):
+        for i, d, p in CHAINS[:4]:
+            if i == h:
+                arriving[h, d, p].wait_recv()
+                ref = slot(h, d, p, chain_length(d, p))
+                total = terms[h, 0, HALVES[p]] + ref[...].astype(jnp.float32)
+                summed[h, HALVES[p]] = total.astype(jnp.bfloat16)
         exchange(
             lambda i: summed.at[h, wrap(across[h] + i + 1)], lambda i: landed.at[h, i],
             sends.at[1], recvs.at[h], [line_device(1 - h, k) for k in range(1, N)],
         )
-    device = line_device(0, 1)
     for h in range(2):
         arrived(landed.at[h], recvs.at[h], sends.at[1], device)
         total = summed[h, across[h]].astype(jnp.float32)
@@ -481,8 +504,9 @@
             total = total + landed[h, i].astype(jnp.float32)
         mine_ref[h] = total.astype(jnp.bfloat16)
 
-    def add_squares(h, index):
-        block = right_ref[h, index].astype(jnp.float32).reshape(N * HALF // N, N, RANK)
+    def add_squares(h, index, part):
+        block = right_ref[h, index, HALVES[part]].astype(jnp.float32)
+        block = block.reshape(HALF // 2, N, RANK)
         squares[...] += jnp.sum(block * block, axis=0)
 
     gather_plane(mine_ref, right_ref, gather_sends, direct, landing, add_squares)
@@ -498,7 +522,7 @@
     for k in range(1, N):
         total = total + spread[k]
     squares_ref[...] = total
-    left_here(chain.at[:, pl.ds(0, N - 1)], sends.at[0], recvs.at[0], device)
+    left_here(chain.at[:, pl.ds(0, N - 2)], sends.at[0], recvs.at[0], device)
     left_here(landed, sends.at[1], recvs.at[0], device)
     left_here(others, sends.at[2], recvs.at[0], device)
 
@@ -516,7 +540,7 @@
         out_specs=(VMEM,) * 3,
         scratch_shapes=[
             pltpu.VMEM((2, 2 * LINKS, N, HALF, RANK), bf16),
-            pltpu.VMEM((4, N, HALF, RANK), f32),
+            pltpu.VMEM((2, 2, N, HALF, RANK), f32),
             pltpu.VMEM((2, N, HALF, RANK), bf16),
             pltpu.VMEM((2, N - 1, HALF, RANK), bf16),
             pltpu.VMEM((N, RANK), f32),
@@ -524,8 +548,8 @@
         ]
         + gather_sems()
         + [
-            pltpu.SemaphoreType.DMA((3,)),
-            pltpu.SemaphoreType.DMA((2, 2, N // 2)),
+            pltpu.SemaphoreType.DMA((4,)),
+            pltpu.SemaphoreType.DMA((2, 2, 2, N // 2)),
             pltpu.SemaphoreType.DMA((3,)),
         ],
         compiler_params=params(1),

time: 162 us -> 152 us (0.938)
  Pallas kernels: 156 us -> 146 us
    pallas_call x1, Pallas kernels: 59.4 us -> 53.2 us  [make_right(): pl.pallas_call(right_kernel, out_shape=(jax.ShapeDtypeStruct((2, HALF, RA...]
    pallas_call x1, Pallas kernels: 74.6 us -> 70.8 us  [front(): pl.pallas_call(front_kernel, out_shape=(jax.ShapeDtypeStruct((rows, RANK)...]
where the time goes in v5:
time: 152 us; the launch traced here: 149 us
  Pallas kernels  146 us (96%)
    pallas_call x1, Pallas kernels, front(): pl.pallas_call(front_kernel, out_shape=(jax.ShapeDtypeStruct((rows, RANK)...  70.8 us
    pallas_call x1, Pallas kernels, make_right(): pl.pallas_call(right_kernel, out_shape=(jax.ShapeDtypeStruct((2, HALF, RA...  53.2 us
    pallas_call x1, Pallas kernels, orthonormalize(): pl.pallas_call(ortho_kernel, out_shape=jax.ShapeDtypeStruct(left.shape, j...  19.8 us

profile of v5, /device:TPU:6, one launch (start us, length us, event | category | flops | bytes accessed | tf_op | source)
XLA Modules:
  0.0 149.4 jit_solution(2867092251126091482)
XLA Ops:
  0.6 0.8 pad.9
  1.4 1.4 fusion
  2.8 0.3 copy.7
  3.0 0.1 reshape.12
  3.1 0.1 fusion.1
  3.2 0.0 copy-start
  3.2 0.0 copy-start.1
  3.2 0.1 pad_maximum_fusion.wide_ref
  3.3 70.8 %front.1 = (f32[128,512]{1,0:T(8,128)S(1)}, f32[512,512]{1,0:T(8,128)S(1)}) custom-call(bf16[2,16,512]{2,1,0:T(8,128)(2,1)S(1)} %bitcast.9, bf16[2,8,8,16,128]{4,3,2,1,0:T(8,128)(2,1)S(1)} %pad_maximum_fusion.wide_ref), custom_call_target="tpu_custom_call" | custom-call | tf_op jit(solution)/shard_map/front/pallas_call | solution.py:263
  74.1 19.8 %orthonormalize.1.ortho_ref = bf16[128,512]{1,0:T(8,128)(2,1)S(1)} custom-call(f32[512,512]{1,0:T(8,128)S(1)} %get-tuple-element.8.gram_ref, f32[128,512]{1,0:T(8,128)S(1)} %get-tuple-element.9.left_ref), custom_call_target="tpu_custom_call" | custom-call | tf_op jit(solution)/shard_map/orthonormalize/pallas_call | solution.py:411
  93.9 53.2 %make_right.1 = (bf16[2,16,512]{2,1,0:T(8,128)(2,1)S(1)}, bf16[2,8,8,16,512]{4,3,2,1,0:T(8,128)(2,1)S(1)}, f32[8,512]{1,0:T(8,128)S(1)}) custom-call(bf16[2,8,8,16,128]{4,3,2,1,0:T(8,128)(2,1)S(1)} %pad_maximum_fusion.wide_ref, bf16[128,512]{1,0:T(8,128)(2,1)S(1)} %orthonormalize.1.ortho_ref), custom_call_target="tpu_custom_call" | custom-call | tf_op jit(solution)/shard_map/make_right/pallas_call | solution.py:532
  147.2 0.0 copy-done
  147.2 0.0 copy-done.1
  147.2 2.2 %finish.1 = (bf16[128,1792]{1,0:T(8,128)(2,1)}, f32[128,1792]{1,0:T(8,128)}, bf16[28,512]{1,0:T(8,128)(2,1)}) custom-call(f32[8,512]{1,0:T(8,128)S(1)} %get-tuple-element.10.squares_ref, bf16[2,8,8,16,512]{4,3,2,1,0:T(8,128)(2,1)S(1)} %get-tuple-element.11.first_ref.second_ref, bf16[2,8,8,16,512]{4,3,2,1,0:T(8,128)(2,1)S(1)} %get-tuple-element.11.first_ref.second_ref, ...), custom_call_target="tpu_custom_call" | custom-call | tf_op jit(solution)/shard_map/finish/pallas_call | solution.py:602
  (1 shorter events, 0.0 us)
Async XLA Ops:
  3.2 144.0 %copy-start = (f32[128,1792]{1,0:T(8,128)S(1)}, f32[128,1792]{1,0:T(8,128)}, u32[]{:S(2)}) copy-start(f32[128,1792]{1,0:T(8,128)} %momentum_ref.1) | copy-start | bytes 2752516
  3.2 144.0 %copy-start.1 = (bf16[128,1792]{1,0:T(8,128)(2,1)S(1)}, bf16[128,1792]{1,0:T(8,128)(2,1)}, u32[]{:S(2)}) copy-start(bf16[128,1792]{1,0:T(8,128)(2,1)} %gradient_ref.1) | copy-start | bytes 1376260

commit v6 on v5

--- a/solution.py
+++ b/solution.py
@@ -15,6 +15,7 @@
 ROWS = 28
 PAD = 32
 HALF = 16
+BLOCK = 128
 MESH = pl.DeviceIdType.MESH
 HIGHEST = lax.Precision.HIGHEST
 VMEM = pl.BlockSpec(memory_space=pltpu.VMEM)
@@ -59,6 +60,13 @@
     return (y * N + wrap(z + offset), tp)
 
 
+def split(rows):
+    rest = jnp.concatenate(
+        [rows[HALF:], jnp.zeros((PAD - ROWS, rows.shape[1]), jnp.float32)], axis=0
+    )
+    return rows[:HALF].astype(jnp.bfloat16), rest.astype(jnp.bfloat16)
+
+
 def tp_device(offset):
     return (lax.axis_index("fsdp"), wrap(lax.axis_index("tp") + offset))
 
@@ -93,7 +101,7 @@
         remote(source(i), target(i), send_sem, recv_sem, device).start()
 
 
-def gather_plane(mine, out, sends, direct, landing, visit):
+def gather_plane(mine, out, sends, direct, landing, visit=None, beside=None):
     y, z, _ = place()
     ring, across = (y, z), (z, y)
     for k in range(1, N):
@@ -104,6 +112,8 @@
             ).start()
     for h in range(2):
         out[h, ring[h], across[h]] = mine[h]
+    if beside is not None:
+        beside(0)
     for h in range(2):
         arrived(
             out.at[h, ring[h], pl.ds(0, N - 1)], direct.at[h], sends.at[0], line_device(1 - h, 1)
@@ -113,8 +123,11 @@
     for step in range(1, N // 2 + 2):
         for h, d, p in CHAINS:
             if step == 1 and (h, d, p) == CHAINS[4]:
-                for i, q in [(0, 0), (0, 1), (1, 0), (1, 1)]:
-                    visit(i, ring[i], q)
+                if visit is not None:
+                    for i, q in [(0, 0), (0, 1), (1, 0), (1, 1)]:
+                        visit(i, ring[i], q)
+                if beside is not None:
+                    beside(1)
                 left_here(out.at[:, 0], sends.at[2], direct.at[0], device)
             if 1 < step <= chain_length(d, p) + 1:
                 arriving[h, d, p].wait_recv()
@@ -125,9 +138,12 @@
                     landing.at[h, d, p, step - 1], line_device(h, signs(d)),
                 )
                 arriving[h, d, p].start()
-        for h, d, p in CHAINS:
-            if 1 < step <= chain_length(d, p) + 1:
-                visit(h, wrap(ring[h] - signs(d) * (step - 1)), p)
+        if visit is not None:
+            for h, d, p in CHAINS:
+                if 1 < step <= chain_length(d, p) + 1:
+                    visit(h, wrap(ring[h] - signs(d) * (step - 1)), p)
+        if beside is not None and step > 1:
+            beside(step)
     left_here(out.at[:, 0, pl.ds(0, N - 1)], sends.at[0], direct.at[0], device)
     left_here(out.at[:, pl.ds(0, N - 2)], sends.at[1], direct.at[0], device)
 
@@ -140,15 +156,26 @@
     ]
 
 
-def front_kernel(
-    factor_ref, wide_ref, left_ref, gram_ref,
-    got, partial_ref, landed, local, first, second, mine, slice_ref,
+def front_part(
+    factor_ref, gradient_ref, momentum_ref, left_ref, gram_ref, wide_ref,
+    turned, got, partial_ref, landed, local, first, second, mine, slice_ref, padded,
     gather_sends, direct, landing, sends, recvs,
 ):
     y, z, tp = place()
     greet_start(all_peers())
     partial_ref[...] = jnp.zeros_like(partial_ref)
+    padded[0], padded[1] = split(factor_ref[...].astype(jnp.float32))
     greet_end(all_peers())
+
+    def arrange(step):
+        if step:
+            return
+        wide = (momentum_ref[...] + gradient_ref[...].astype(jnp.float32)).astype(jnp.bfloat16)
+        turned[...] = wide.astype(jnp.float32).T
+        for i in range(N):
+            for j in range(N):
+                at = (i * N + j) * ROWS
+                wide_ref[0, i, j], wide_ref[1, j, i] = split(turned[at : at + ROWS, :])
 
     def add_terms(h, index, part):
         block = wide_ref[h, index, HALVES[part]].reshape(N // 2 * HALF, wide_ref.shape[-1])
@@ -157,7 +184,7 @@
             block, rows, (((0,), (0,)), ((), ())), preferred_element_type=jnp.float32
         )
 
-    gather_plane(factor_ref, got, gather_sends, direct, landing, add_terms)
+    gather_plane(padded, got, gather_sends, direct, landing, add_terms, arrange)
 
     def rows(index):
         return pl.ds(pl.multiple_of(index * HALF, HALF), HALF)
@@ -257,35 +284,6 @@
     left_here(gram_ref.at[pl.ds(0, (N - 1) * size)], sends.at[5], recvs.at[0], sibling)
 
 
-def front(factor, wide):
-    rows = wide.shape[-1]
-    f32 = jnp.float32
-    return pl.pallas_call(
-        front_kernel,
-        out_shape=(
-            jax.ShapeDtypeStruct((rows, RANK), f32),
-            jax.ShapeDtypeStruct((RANK, RANK), f32),
-        ),
-        in_specs=[VMEM, VMEM],
-        out_specs=(VMEM, VMEM),
-        scratch_shapes=[
-            pltpu.VMEM((2, N, N, HALF, RANK), jnp.bfloat16),
-            pltpu.VMEM((rows, RANK), f32),
-            pltpu.VMEM((N - 1, HALF, RANK), f32),
-            pltpu.VMEM((BLOCK, RANK), f32),
-            pltpu.VMEM((2, N - 1, N, RANK // 2), f32),
-            pltpu.VMEM((2, N, N, RANK // 2), f32),
-            pltpu.VMEM((2, N, RANK // 2), f32),
-            pltpu.VMEM((RANK // N, RANK), f32),
-        ]
-        + gather_sems()
-        + [pltpu.SemaphoreType.DMA((6,)), pltpu.SemaphoreType.DMA((13,))],
-        compiler_params=params(0),
-        name="front",
-    )(factor, wide)
-
-
-BLOCK = 128
 BASE = 8
 
 
@@ -388,9 +386,7 @@
     )
 
 
-def ortho_kernel(gram_ref, left_ref, out_ref, rest, tail):
-    rest[...] = gram_ref[...]
-    tail[...] = left_ref[...]
+def ortho_part(rest, tail, out_ref):
     for at in range(0, RANK, BLOCK):
         end = at + BLOCK
         inverse = block_inverse(rest[at:end, at:end])
@@ -407,32 +403,16 @@
         tail[:, end:] -= full_dot(done, panel, ((1,), (0,)))
 
 
-def orthonormalize(gram, left):
-    return pl.pallas_call(
-        ortho_kernel,
-        out_shape=jax.ShapeDtypeStruct(left.shape, jnp.bfloat16),
-        in_specs=[VMEM, VMEM],
-        out_specs=VMEM,
-        scratch_shapes=[
-            pltpu.VMEM((RANK, RANK), jnp.float32),
-            pltpu.VMEM(left.shape, jnp.float32),
-        ],
-        compiler_params=pltpu.CompilerParams(vmem_limit_bytes=48 * 2**20),
-        name="orthonormalize",
-    )(gram, left)
-
-
 LINKS = N // 2 + 1
 
 
-def right_kernel(
+def right_part(
     wide_ref, ortho_ref, mine_ref, right_ref, squares_ref,
-    chain, terms, summed, landed, squares, spread,
+    chain, terms, summed, landed, squares, over_tp, over_line,
     gather_sends, direct, landing, sends, chain_recv, recvs,
 ):
     y, z, tp = place()
     ring, across = (y, z), (z, y)
-    greet_start(all_peers())
 
     def own(h, target, part):
         block = wide_ref[h, wrap(target), HALVES[part]]
@@ -464,8 +444,6 @@
     for h, d, p in CHAINS:
         term = own(h, ring[h] + signs(d) * chain_length(d, p), p)
         slot(h, d, p, 0)[...] = term.astype(jnp.bfloat16)
-    squares[...] = jnp.zeros_like(squares)
-    greet_end(all_peers())
     device = line_device(0, 1)
     for h, d, p in CHAINS[:4]:
         pass_on(h, d, p, 1)
@@ -504,64 +482,119 @@
             total = total + landed[h, i].astype(jnp.float32)
         mine_ref[h] = total.astype(jnp.bfloat16)
 
-    def add_squares(h, index, part):
-        block = right_ref[h, index, HALVES[part]].astype(jnp.float32)
-        block = block.reshape(HALF // 2, N, RANK)
-        squares[...] += jnp.sum(block * block, axis=0)
-
-    gather_plane(mine_ref, right_ref, gather_sends, direct, landing, add_squares)
-
-    exchange(
-        lambda i: squares, lambda i: spread.at[tp], sends.at[2], recvs.at[2],
-        [tp_device(k) for k in range(1, N)],
-    )
-    spread[tp] = squares[...]
-    others = spread.at[pl.ds(0, N - 1)]
-    arrived(others, recvs.at[2], sends.at[2], device)
-    total = spread[0]
-    for k in range(1, N):
-        total = total + spread[k]
+    def add_squares(step):
+        if step == 1:
+            for h in range(2):
+                block = right_ref[h, ring[h]].astype(jnp.float32).reshape(N * HALF // N, N, RANK)
+                total = jnp.sum(jnp.sum(block * block, axis=0), axis=0, keepdims=True)
+                pieces = [total[:, c : c + BLOCK] for c in range(0, RANK, BLOCK)]
+                pieces.append(jnp.zeros((N - len(pieces), BLOCK), jnp.float32))
+                squares[h] = jnp.concatenate(pieces, axis=0)
+            over_tp[tp] = squares[...]
+            exchange(
+                lambda i: squares, lambda i: over_tp.at[tp], sends.at[2], recvs.at[2],
+                [tp_device(k) for k in range(1, N)],
+            )
+        if step == 3:
+            arrived(over_tp.at[pl.ds(0, N - 1)], recvs.at[2], sends.at[2], device)
+            total = over_tp[0]
+            for k in range(1, N):
+                total = total + over_tp[k]
+            for h in range(2):
+                over_line[h, ring[h]] = total[h]
+                ref = over_line.at[h, ring[h]]
+                exchange(
+                    lambda i: ref, lambda i: ref, sends.at[4], recvs.at[3 + h],
+                    [line_device(h, k) for k in range(1, N)],
+                )
+
+    gather_plane(
+        mine_ref, right_ref, gather_sends, direct, landing, beside=add_squares
+    )
+    total = jnp.zeros((N, BLOCK), jnp.float32)
+    for h in range(2):
+        arrived(over_line.at[h, pl.ds(0, N - 1)], recvs.at[3 + h], sends.at[4], device)
+        for k in range(N):
+            total = total + over_line[h, k]
     squares_ref[...] = total
     left_here(chain.at[:, pl.ds(0, N - 2)], sends.at[0], recvs.at[0], device)
     left_here(landed, sends.at[1], recvs.at[0], device)
-    left_here(others, sends.at[2], recvs.at[0], device)
-
-
-def make_right(wide, ortho):
+    left_here(over_tp.at[pl.ds(0, N - 1)], sends.at[2], recvs.at[0], device)
+    left_here(over_line.at[:, pl.ds(0, N - 1)], sends.at[4], recvs.at[0], device)
+
+
+FRONT_SCRATCH = [
+    pltpu.VMEM((FFW // N, BLOCK), jnp.float32),
+    pltpu.VMEM((2, N, N, HALF, RANK), jnp.bfloat16),
+    pltpu.VMEM((BLOCK, RANK), jnp.float32),
+    pltpu.VMEM((N - 1, HALF, RANK), jnp.float32),
+    pltpu.VMEM((BLOCK, RANK), jnp.float32),
+    pltpu.VMEM((2, N - 1, N, RANK // 2), jnp.float32),
+    pltpu.VMEM((2, N, N, RANK // 2), jnp.float32),
+    pltpu.VMEM((2, N, RANK // 2), jnp.float32),
+    pltpu.VMEM((RANK // N, RANK), jnp.float32),
+    pltpu.VMEM((2, HALF, RANK), jnp.bfloat16),
+    *gather_sems(),
+    pltpu.SemaphoreType.DMA((6,)),
+    pltpu.SemaphoreType.DMA((13,)),
+]
+
+
+RIGHT_SCRATCH = [
+    pltpu.VMEM((2, 2 * LINKS, N, HALF, RANK), jnp.bfloat16),
+    pltpu.VMEM((2, 2, N, HALF, RANK), jnp.float32),
+    pltpu.VMEM((2, N, HALF, RANK), jnp.bfloat16),
+    pltpu.VMEM((2, N - 1, HALF, RANK), jnp.bfloat16),
+    pltpu.VMEM((2, N, BLOCK), jnp.float32),
+    pltpu.VMEM((N, 2, N, BLOCK), jnp.float32),
+    pltpu.VMEM((2, N, N, BLOCK), jnp.float32),
+    *gather_sems(),
+    pltpu.SemaphoreType.DMA((5,)),
+    pltpu.SemaphoreType.DMA((2, 2, 2, N // 2)),
+    pltpu.SemaphoreType.DMA((5,)),
+]
+
+
+def step_kernel(
+    factor_ref, gradient_ref, momentum_ref, ortho_ref, mine_ref, right_ref, squares_ref,
+    left, gram, wide, *scratch,
+):
+    count = len(FRONT_SCRATCH)
+    front_part(factor_ref, gradient_ref, momentum_ref, left, gram, wide, *scratch[:count])
+    ortho_part(gram, left, ortho_ref)
+    right_part(wide, ortho_ref, mine_ref, right_ref, squares_ref, *scratch[count:])
+
+
+def make_right(factor, gradient, momentum):
+    rows = gradient.shape[0]
     f32, bf16 = jnp.float32, jnp.bfloat16
     return pl.pallas_call(
-        right_kernel,
+        step_kernel,
         out_shape=(
+            jax.ShapeDtypeStruct((rows, RANK), bf16),
             jax.ShapeDtypeStruct((2, HALF, RANK), bf16),
             jax.ShapeDtypeStruct((2, N, N, HALF, RANK), bf16),
-            jax.ShapeDtypeStruct((N, RANK), f32),
+            jax.ShapeDtypeStruct((N, BLOCK), f32),
         ),
-        in_specs=[VMEM] * 2,
-        out_specs=(VMEM,) * 3,
+        in_specs=[VMEM] * 3,
+        out_specs=(VMEM,) * 4,
         scratch_shapes=[
-            pltpu.VMEM((2, 2 * LINKS, N, HALF, RANK), bf16),
-            pltpu.VMEM((2, 2, N, HALF, RANK), f32),
-            pltpu.VMEM((2, N, HALF, RANK), bf16),
-            pltpu.VMEM((2, N - 1, HALF, RANK), bf16),
-            pltpu.VMEM((N, RANK), f32),
-            pltpu.VMEM((N, N, RANK), f32),
+            pltpu.VMEM((rows, RANK), f32),
+            pltpu.VMEM((RANK, RANK), f32),
+            pltpu.VMEM((2, N, N, HALF, rows), bf16),
         ]
-        + gather_sems()
-        + [
-            pltpu.SemaphoreType.DMA((4,)),
-            pltpu.SemaphoreType.DMA((2, 2, 2, N // 2)),
-            pltpu.SemaphoreType.DMA((3,)),
-        ],
-        compiler_params=params(1),
+        + FRONT_SCRATCH
+        + RIGHT_SCRATCH,
+        compiler_params=params(0),
         name="make_right",
-    )(wide, ortho)
+    )(factor, gradient, momentum)
 
 
 def finish_kernel(
     squares_ref, first_ref, second_ref, mine_ref, ortho_ref, gradient_ref, momentum_ref,
     update_ref, new_ref, factor_ref, factor,
 ):
-    squares = jnp.sum(squares_ref[...], axis=0, keepdims=True)
+    squares = jnp.concatenate([squares_ref[c : c + 1, :] for c in range(RANK // BLOCK)], axis=1)
     norms = jnp.sqrt(squares + 1e-06)
     gain = math.sqrt(FFW) / norms
     ortho = ortho_ref[...]
@@ -608,7 +641,7 @@
             jax.ShapeDtypeStruct((ROWS, RANK), jnp.bfloat16),
         ),
         in_specs=[
-            whole(N, RANK),
+            whole(N, BLOCK),
             pl.BlockSpec((1, some, N, HALF, RANK), lambda i: (0, i, 0, 0, 0)),
             pl.BlockSpec((1, N, some, HALF, RANK), lambda i: (1, 0, i, 0, 0)),
             whole(2, HALF, RANK),
@@ -624,15 +657,7 @@
 
 
 def body(gradient, momentum, right_factor):
-    wide = (momentum + gradient.astype(jnp.float32)).astype(jnp.bfloat16)
-    row_count = wide.shape[0]
-    blocks = wide.T.reshape(N, N, ROWS, row_count)
-    blocks = jnp.pad(blocks, ((0, 0), (0, 0), (0, PAD - ROWS), (0, 0)))
-    blocks = jnp.stack([blocks[:, :, :HALF], jnp.swapaxes(blocks[:, :, HALF:], 0, 1)])
-    factor = jnp.pad(right_factor, ((0, PAD - ROWS), (0, 0))).reshape(2, HALF, RANK)
-    left, gram = front(factor, blocks)
-    ortho = orthonormalize(gram, left)
-    mine, right, squares = make_right(blocks, ortho)
+    ortho, mine, right, squares = make_right(right_factor, gradient, momentum)
     return finish(squares, right, mine, ortho, gradient, momentum)
 
 

time: 152 us -> 146 us (0.961); the launches traced: 149 us -> 146 us
  Pallas kernels: 146 us -> 140 us
  local copies, waits for them, and re-layouts: 1.19 us -> 5.14 us
    pallas_call x3 -> x1, Pallas kernels: 144 us -> 138 us  [make_right(): pl.pallas_call(step_kernel, out_shape=(jax.ShapeDtypeStruct((rows, RANK),...]
    unnamed x4 -> x10, local copies, waits for them, and re-layouts: 0.01 us -> 5.14 us
where the time goes in v6:
time: 146 us
  Pallas kernels  140 us (96%)
  local copies, waits for them, and re-layouts  5.14 us (4%)
    pallas_call x1, Pallas kernels, make_right(): pl.pallas_call(step_kernel, out_shape=(jax.ShapeDtypeStruct((rows, RANK),...  138 us
    unnamed x10, local copies, waits for them, and re-layouts  5.14 us

profile of v6, /device:TPU:6, one launch (start us, length us, event | category | flops | bytes accessed | tf_op | source)
XLA Modules:
  0.0 146.1 jit_solution(16572718739878410922)
XLA Ops:
  0.6 0.0 copy-start
  0.6 1.2 copy-done
  1.8 0.0 copy-start.2
  1.8 1.0 copy-done.2
  2.8 0.0 copy-start.4
  2.8 0.8 copy-done.4
  3.6 138.2 %make_right.1 = (bf16[128,512]{1,0:T(8,128)(2,1)S(1)}, bf16[2,16,512]{2,1,0:T(8,128)(2,1)S(1)}, bf16[2,8,8,16,512]{4,3,2,1,0:T(8,128)(2,1)S(1)}, f32[8,128]{1,0:T(8,128)S(1)}) custom-call(bf16[28,512]{1,0:T(8,128)(2,1)S(1)} %copy-done.4, bf16[128,1792]{1,0:T(8,128)(2,1)S(1)} %copy-done.2, f32[128,1792]{1,0:T(8,128)S(1)} %copy-done), custom_call_target="tpu_custom_call" | custom-call | tf_op jit(solution)/shard_map/make_right/pallas_call | solution.py:571
  141.8 0.0 copy-start.1
  141.8 1.2 copy-done.1
  143.0 0.0 copy-start.3
  143.0 1.0 copy-done.3
  144.0 2.1 %finish.1 = (bf16[128,1792]{1,0:T(8,128)(2,1)}, f32[128,1792]{1,0:T(8,128)}, bf16[28,512]{1,0:T(8,128)(2,1)}) custom-call(f32[8,128]{1,0:T(8,128)S(1)} %get-tuple-element.7.squares_ref, bf16[2,8,8,16,512]{4,3,2,1,0:T(8,128)(2,1)S(1)} %get-tuple-element.8.first_ref.second_ref, bf16[2,8,8,16,512]{4,3,2,1,0:T(8,128)(2,1)S(1)} %get-tuple-element.8.first_ref.second_ref, ...), custom_call_target="tpu_custom_call" | custom-call | tf_op jit(solution)/shard_map/finish/pallas_call | solution.py:635
Async XLA Ops:
  0.6 1.2 copy-start
  1.8 1.0 copy-start.2
  2.8 0.8 copy-start.4
  141.8 1.2 copy-start.1
  143.0 1.0 copy-start.3

commit v7 on v6

--- a/solution.py
+++ b/solution.py
@@ -157,7 +157,7 @@
 
 
 def front_part(
-    factor_ref, gradient_ref, momentum_ref, left_ref, gram_ref, wide_ref,
+    factor_ref, whole_ref, left_ref, gram_ref, wide_ref,
     turned, got, partial_ref, landed, local, first, second, mine, slice_ref, padded,
     gather_sends, direct, landing, sends, recvs,
 ):
@@ -170,8 +170,7 @@
     def arrange(step):
         if step:
             return
-        wide = (momentum_ref[...] + gradient_ref[...].astype(jnp.float32)).astype(jnp.bfloat16)
-        turned[...] = wide.astype(jnp.float32).T
+        turned[...] = whole_ref[...].astype(jnp.bfloat16).astype(jnp.float32).T
         for i in range(N):
             for j in range(N):
                 at = (i * N + j) * ROWS
@@ -556,17 +555,17 @@
 
 
 def step_kernel(
-    factor_ref, gradient_ref, momentum_ref, ortho_ref, mine_ref, right_ref, squares_ref,
+    factor_ref, whole_ref, ortho_ref, mine_ref, right_ref, squares_ref,
     left, gram, wide, *scratch,
 ):
     count = len(FRONT_SCRATCH)
-    front_part(factor_ref, gradient_ref, momentum_ref, left, gram, wide, *scratch[:count])
+    front_part(factor_ref, whole_ref, left, gram, wide, *scratch[:count])
     ortho_part(gram, left, ortho_ref)
     right_part(wide, ortho_ref, mine_ref, right_ref, squares_ref, *scratch[count:])
 
 
-def make_right(factor, gradient, momentum):
-    rows = gradient.shape[0]
+def make_right(factor, whole):
+    rows = whole.shape[0]
     f32, bf16 = jnp.float32, jnp.bfloat16
     return pl.pallas_call(
         step_kernel,
@@ -576,7 +575,7 @@
             jax.ShapeDtypeStruct((2, N, N, HALF, RANK), bf16),
             jax.ShapeDtypeStruct((N, BLOCK), f32),
         ),
-        in_specs=[VMEM] * 3,
+        in_specs=[VMEM] * 2,
         out_specs=(VMEM,) * 4,
         scratch_shapes=[
             pltpu.VMEM((rows, RANK), f32),
@@ -587,11 +586,11 @@
         + RIGHT_SCRATCH,
         compiler_params=params(0),
         name="make_right",
-    )(factor, gradient, momentum)
+    )(factor, whole)
 
 
 def finish_kernel(
-    squares_ref, first_ref, second_ref, mine_ref, ortho_ref, gradient_ref, momentum_ref,
+    squares_ref, first_ref, second_ref, mine_ref, ortho_ref, whole_ref,
     update_ref, new_ref, factor_ref, factor,
 ):
     squares = jnp.concatenate([squares_ref[c : c + 1, :] for c in range(RANK // BLOCK)], axis=1)
@@ -622,13 +621,12 @@
     )
     rows = ortho.shape[0]
     update_ref[...] = (math.sqrt(D / RANK) * combined[:rows]).astype(jnp.bfloat16)
-    whole = momentum_ref[...] + gradient_ref[...].astype(jnp.float32)
-    new_ref[...] = whole - 0.05 * combined[rows:]
-
-
-def finish(squares, right, mine, ortho, gradient, momentum):
+    new_ref[...] = whole_ref[...] - 0.05 * combined[rows:]
+
+
+def finish(squares, right, mine, ortho, summed):
     steps = 2
-    rows, columns = gradient.shape
+    rows, columns = summed.shape
     some = N // steps
     whole = lambda *shape: pl.BlockSpec(shape, lambda i: (0,) * len(shape))
     tile = pl.BlockSpec((rows, columns // steps), lambda i: (0, i))
@@ -647,18 +645,18 @@
             whole(2, HALF, RANK),
             whole(rows, RANK),
             tile,
-            tile,
         ],
         out_specs=(tile, tile, whole(ROWS, RANK)),
         scratch_shapes=[pltpu.VMEM((columns // steps, RANK), jnp.bfloat16)],
         compiler_params=pltpu.CompilerParams(vmem_limit_bytes=48 * 2**20),
         name="finish",
-    )(squares, right, right, mine, ortho, gradient, momentum)
+    )(squares, right, right, mine, ortho, summed)
 
 
 def body(gradient, momentum, right_factor):
-    ortho, mine, right, squares = make_right(right_factor, gradient, momentum)
-    return finish(squares, right, mine, ortho, gradient, momentum)
+    whole = momentum + gradient.astype(jnp.float32)
+    ortho, mine, right, squares = make_right(right_factor, whole)
+    return finish(squares, right, mine, ortho, whole)
 
 
 def solution(mesh):

time: 146 us -> 142 us (0.973)
  local copies, waits for them, and re-layouts: 5.14 us -> 0.01 us
    unnamed x10 -> x2, local copies, waits for them, and re-layouts: 5.14 us -> 0.01 us
where the time goes in v7:
time: 142 us
  Pallas kernels  140 us (99%)
    pallas_call x1, Pallas kernels, make_right(): pl.pallas_call(step_kernel, out_shape=(jax.ShapeDtypeStruct((rows, RANK),...  138 us

profile of v7, /device:TPU:6, one launch (start us, length us, event | category | flops | bytes accessed | tf_op | source)
XLA Modules:
  0.0 142.1 jit_solution(16889716391721427458)
XLA Ops:
  0.6 0.0 copy-start
  0.6 1.4 convert_add_fusion.whole_ref
  2.0 0.0 copy-done
  2.0 138.0 %make_right.1 = (bf16[128,512]{1,0:T(8,128)(2,1)S(1)}, bf16[2,16,512]{2,1,0:T(8,128)(2,1)S(1)}, bf16[2,8,8,16,512]{4,3,2,1,0:T(8,128)(2,1)S(1)}, f32[8,128]{1,0:T(8,128)S(1)}) custom-call(bf16[28,512]{1,0:T(8,128)(2,1)S(1)} %copy-done, f32[128,1792]{1,0:T(8,128)S(1)} %convert_add_fusion.whole_ref), custom_call_target="tpu_custom_call" | custom-call | tf_op jit(solution)/shard_map/make_right/pallas_call | solution.py:570
  140.0 2.1 %finish.1 = (bf16[128,1792]{1,0:T(8,128)(2,1)}, f32[128,1792]{1,0:T(8,128)}, bf16[28,512]{1,0:T(8,128)(2,1)}) custom-call(f32[8,128]{1,0:T(8,128)S(1)} %get-tuple-element.7.squares_ref, bf16[2,8,8,16,512]{4,3,2,1,0:T(8,128)(2,1)S(1)} %get-tuple-element.8.first_ref.second_ref, bf16[2,8,8,16,512]{4,3,2,1,0:T(8,128)(2,1)S(1)} %get-tuple-element.8.first_ref.second_ref, ...), custom_call_target="tpu_custom_call" | custom-call | tf_op jit(solution)/shard_map/finish/pallas_call | solution.py:633
Async XLA Ops:
  0.6 1.4 copy-start
